TPU v7x, 32 devices: a whole 2x2x4 slice. The times are simulated.
32 devices in a mesh: fsdp: 4 (over z), heads: 2 (over core), tensor: 4 (over y, x).
Axes of the slice: x: 2, y: 2, z: 4, core: 2. Of those that a mesh axis runs over, the one named last changes fastest.
Arguments:
- tokens: bfloat16 [16, 1024, 1152], P(('fsdp', 'tensor'), 'heads'), may hold values from -6 to 6
- seq_lens: int32 [16, 8], P(('fsdp', 'tensor')), may hold values from 0 to 1024, as said below
- cotangent: bfloat16 [16, 1024, 1152], P(('fsdp', 'tensor'), 'heads'), may hold values from -6 to 6
- w_query: bfloat16 [1152, 1152], P(('fsdp', 'tensor'), 'heads'), may hold values from -0.1875 to 0.1875
- w_key: bfloat16 [1152, 384], P(('fsdp', 'tensor'), 'heads'), may hold values from -0.1875 to 0.1875
- w_value: bfloat16 [1152, 384], P(('fsdp', 'tensor'), 'heads'), may hold values from -0.1875 to 0.1875
- w_out: bfloat16 [1152, 1152], P('heads', ('fsdp', 'tensor')), may hold values from -1.5 to 1.5
- norm_first: bfloat16 [1152], P(('fsdp', 'tensor')), may hold values from 0.5 to 1.5
- norm_second: bfloat16 [1152], P(('fsdp', 'tensor')), may hold values from 0.5 to 1.5
- w_gate: bfloat16 [1152, 3072], P(('fsdp', 'heads'), 'tensor'), may hold values from -0.1875 to 0.1875
- w_up: bfloat16 [1152, 3072], P(('fsdp', 'heads'), 'tensor'), may hold values from -0.1875 to 0.1875
- w_down: bfloat16 [3072, 1152], P('tensor', ('fsdp', 'heads')), may hold values from -0.109375 to 0.109375
Outputs:
- layer_out: bfloat16 [16, 1024, 1152], P(('fsdp', 'tensor'), 'heads')
- grad_tokens: float32 [16, 1024, 1152], P(('fsdp', 'tensor'), 'heads')
- grad_query: float32 [1152, 1152], P(('fsdp', 'tensor'), 'heads')
- grad_key: float32 [1152, 384], P(('fsdp', 'tensor'), 'heads')
- grad_value: float32 [1152, 384], P(('fsdp', 'tensor'), 'heads')
- grad_out: float32 [1152, 1152], P('heads', ('fsdp', 'tensor'))
- grad_norm_first: float32 [1152], P(('fsdp', 'tensor'))
- grad_norm_second: float32 [1152], P(('fsdp', 'tensor'))
- grad_gate: float32 [1152, 3072], P(('fsdp', 'heads'), 'tensor')
- grad_up: float32 [1152, 3072], P(('fsdp', 'heads'), 'tensor')
- grad_down: float32 [3072, 1152], P('tensor', ('fsdp', 'heads'))
Inputs may be any that keep to these rules, and one draw needn't show every extreme that they name: `seq_lens`: each row lists the lengths of up to 8 sequences packed from the block's start, zero for an empty slot; a row sums to at most 1024; in every draw some block holds a single sequence of 1024.
All inputs are finite; a program needn't handle non-finite values.
Results may differ from a plain program's by a relative error of at most 0.02.
Values may be sent and summed in bfloat16 or wider, within the bound.
A program may use at most 128 MiB of HBM per device.

v0:
```python
import jax
import jax.numpy as jnp
from jax import lax
from jax.sharding import PartitionSpec as P

HQ = 18
KVH = 6
HD = 64


epsilon = 1e-05
theta_base = 10000.0
mask_fill = -1e30


def contract_rows(left_side, right_side):
    return lax.dot_general(
        left_side, right_side, (((0,), (0,)), ((), ())), preferred_element_type=jnp.float32
    )


def contract_last(left_side, right_side):
    return lax.dot_general(
        left_side, right_side, (((1,), (1,)), ((), ())), preferred_element_type=jnp.float32
    )


def rms_scale(values):
    return lax.rsqrt(jnp.mean(values * values, axis=-1, keepdims=True) + epsilon)


def norm_back(values, inverse_rms, gains, upstream):
    weighted = gains * upstream
    cubed = inverse_rms * inverse_rms * inverse_rms
    return inverse_rms * weighted - values * cubed * jnp.mean(
        values * weighted, axis=-1, keepdims=True
    )


def positions(seq_lens, length):
    ending = jnp.cumsum(seq_lens, axis=1)
    places = jnp.arange(length, dtype=jnp.int32)
    passed = places[None, :, None] >= ending[:, None, :]
    segment = jnp.sum(passed.astype(jnp.int32), axis=2)
    starts = jnp.sum(jnp.where(passed, seq_lens[:, None, :], 0), axis=2)
    return (segment, places[None, :] - starts)


def rotary(offset, head_size):
    half_size = head_size // 2
    frequency = theta_base ** (-2.0 * jnp.arange(half_size, dtype=jnp.float32) / head_size)
    angles = offset.astype(jnp.float32)[..., None] * frequency
    angles = jnp.concatenate([angles, angles], axis=-1)[:, :, None, :]
    return (jnp.cos(angles), jnp.sin(angles))


def rotate(values, cosine, sines):
    half_size = values.shape[-1] // 2
    rotated = jnp.concatenate([-values[..., half_size:], values[..., :half_size]], axis=-1)
    return values * cosine + rotated * sines


def rotate_back(upstream, cosine, sines):
    half_size = upstream.shape[-1] // 2
    scaled = upstream * sines
    return upstream * cosine + jnp.concatenate(
        [scaled[..., half_size:], -scaled[..., :half_size]], axis=-1
    )


def tile_scores(query_tile, key_tile, allowed, factor):
    scores = (
        jnp.einsum("gqd,kd->gqk", query_tile, key_tile, preferred_element_type=jnp.float32) * factor
    )
    return jnp.where(allowed[None], scores, mask_fill)


def tile_forward(query_tile, key_tile, value_tile, allowed, factor):
    scores = tile_scores(query_tile, key_tile, allowed, factor)
    largest = jnp.max(scores, axis=-1, keepdims=True)
    raised = jnp.exp(scores - largest)
    totals = jnp.sum(raised, axis=-1, keepdims=True)
    weights = (raised / totals).astype(jnp.bfloat16)
    output = jnp.einsum("gqk,kd->gqd", weights, value_tile, preferred_element_type=jnp.float32)
    return (output, (largest + jnp.log(totals))[..., 0])


def tile_backward(query_tile, key_tile, value_tile, allowed, logsum, grad_tile, factor):
    scores = tile_scores(query_tile, key_tile, allowed, factor)
    chances = jnp.exp(scores - logsum[..., None])
    chance_grad = jnp.einsum(
        "gqd,kd->gqk", grad_tile, value_tile, preferred_element_type=jnp.float32
    )
    centre = jnp.sum(chances * chance_grad, axis=-1, keepdims=True)
    score_grad = (chances * (chance_grad - centre)).astype(jnp.bfloat16)
    query_grad = (
        jnp.einsum("gqk,kd->gqd", score_grad, key_tile, preferred_element_type=jnp.float32) * factor
    )
    key_grad = (
        jnp.einsum("gqk,gqd->kd", score_grad, query_tile, preferred_element_type=jnp.float32)
        * factor
    )
    value_grad = jnp.einsum(
        "gqk,gqd->kd", chances.astype(jnp.bfloat16), grad_tile, preferred_element_type=jnp.float32
    )
    return (query_grad, key_grad, value_grad)


def local(
    tokens,
    seq_lens,
    cotangent,
    w_query,
    w_key,
    w_value,
    w_out,
    norm_first,
    norm_second,
    w_gate,
    w_up,
    w_down,
):
    blocks, half_len, model_width = tokens.shape
    head_count = lax.axis_size("heads")
    length = half_len * head_count
    head_size = HD
    group_size = HQ // KVH
    query_heads_local = w_query.shape[1] // head_size
    key_heads_local = w_key.shape[1] // head_size
    factor = head_size ** (-0.5)
    query_w, key_w, value_w, out_w, gain_one, gain_two = (
        lax.all_gather(w_query, ("fsdp", "tensor"), axis=0, tiled=True),
        lax.all_gather(w_key, ("fsdp", "tensor"), axis=0, tiled=True),
        lax.all_gather(w_value, ("fsdp", "tensor"), axis=0, tiled=True),
        lax.all_gather(w_out, ("fsdp", "tensor"), axis=1, tiled=True),
        lax.all_gather(norm_first, ("fsdp", "tensor"), axis=0, tiled=True),
        lax.all_gather(norm_second, ("fsdp", "tensor"), axis=0, tiled=True),
    )
    gain_one = gain_one.astype(jnp.float32)
    gain_two = gain_two.astype(jnp.float32)
    gate_w, up_w, down_w = (
        lax.all_gather(w_gate, ("fsdp", "heads"), axis=0, tiled=True),
        lax.all_gather(w_up, ("fsdp", "heads"), axis=0, tiled=True),
        lax.all_gather(w_down, ("fsdp", "heads"), axis=1, tiled=True),
    )
    gathered_rows = lax.all_gather(tokens, "heads", axis=1, tiled=True)
    rows_one = gathered_rows.astype(jnp.float32).reshape(blocks * length, model_width)
    scale_one = rms_scale(rows_one)
    normed_one = (rows_one * scale_one * gain_one).astype(jnp.bfloat16)
    query_raw = jnp.dot(normed_one, query_w, preferred_element_type=jnp.float32)
    key_raw = jnp.dot(normed_one, key_w, preferred_element_type=jnp.float32)
    value_raw = jnp.dot(normed_one, value_w, preferred_element_type=jnp.float32)
    segment, offset = positions(seq_lens, length)
    cosine, sines = rotary(offset, head_size)
    queries = rotate(
        query_raw.reshape(blocks, length, query_heads_local, head_size), cosine, sines
    ).astype(jnp.bfloat16)
    keys = rotate(
        key_raw.reshape(blocks, length, key_heads_local, head_size), cosine, sines
    ).astype(jnp.bfloat16)
    values = value_raw.astype(jnp.bfloat16).reshape(blocks, length, key_heads_local, head_size)
    query_tiles = queries.reshape(blocks, length, key_heads_local, group_size, head_size).transpose(
        0, 2, 3, 1, 4
    )
    key_tiles = keys.transpose(0, 2, 1, 3)
    value_tiles = values.transpose(0, 2, 1, 3)
    tile_rows = min(512, length)
    tile_count = length // tile_rows
    total_tiles = blocks * key_heads_local * tile_count
    places = jnp.arange(length, dtype=jnp.int32)

    def pick(tile_index):
        block_at = tile_index // (key_heads_local * tile_count)
        kv_head = tile_index // tile_count % key_heads_local
        first_row = tile_index % tile_count * tile_rows
        zero = jnp.int32(0)
        query_tile = lax.dynamic_slice(
            query_tiles,
            (block_at, kv_head, zero, first_row, zero),
            (1, 1, group_size, tile_rows, head_size),
        )[0, 0]
        key_tile = lax.dynamic_slice(
            key_tiles, (block_at, kv_head, zero, zero), (1, 1, length, head_size)
        )[0, 0]
        value_tile = lax.dynamic_slice(
            value_tiles, (block_at, kv_head, zero, zero), (1, 1, length, head_size)
        )[0, 0]
        seg_row = segment[0]
        seg_query = lax.dynamic_slice_in_dim(seg_row, first_row, tile_rows)
        rows_at = first_row + jnp.arange(tile_rows, dtype=jnp.int32)
        allowed = (seg_query[:, None] == seg_row[None, :]) & (places[None, :] <= rows_at[:, None])
        return (query_tile, key_tile, value_tile, allowed)

    def forward_tile(tile_index):
        query_tile, key_tile, value_tile, allowed = pick(tile_index)
        return tile_forward(query_tile, key_tile, value_tile, allowed, factor)

    tile_ids = jnp.arange(total_tiles, dtype=jnp.int32)
    tile_outputs, logsums = lax.map(forward_tile, tile_ids)
    attended = tile_outputs.reshape(
        blocks, key_heads_local, tile_count, group_size, tile_rows, head_size
    )
    attended = attended.transpose(0, 2, 4, 1, 3, 5).reshape(
        blocks * length, query_heads_local * head_size
    )
    attended_low = attended.astype(jnp.bfloat16)
    attn_part = jnp.dot(attended_low, out_w, preferred_element_type=jnp.float32).reshape(
        blocks, length, model_width
    )
    mixed = lax.psum_scatter(
        attn_part.astype(jnp.bfloat16), "heads", scatter_dimension=1, tiled=True
    ).astype(jnp.float32)
    residual = (tokens.astype(jnp.float32) + mixed).reshape(blocks * half_len, model_width)
    scale_two = rms_scale(residual)
    normed_two = (residual * scale_two * gain_two).astype(jnp.bfloat16)
    own_rows = normed_two.shape[0]
    down_grad = cotangent.reshape(own_rows, model_width)
    gate_all, up_all, down_all = (gate_w, up_w, down_w)
    ffn_in = lax.all_gather(normed_two, "tensor", axis=0, tiled=True)
    gate_pre = jnp.dot(ffn_in, gate_all, preferred_element_type=jnp.float32)
    up_pre = jnp.dot(ffn_in, up_all, preferred_element_type=jnp.float32)
    sigmoid_gate = jax.nn.sigmoid(gate_pre)
    silu_gate = gate_pre * sigmoid_gate
    hidden = (silu_gate * up_pre).astype(jnp.bfloat16)
    branch = lax.psum_scatter(
        jnp.dot(hidden, down_all, preferred_element_type=jnp.float32).astype(jnp.bfloat16),
        "tensor",
        scatter_dimension=0,
        tiled=True,
    ).astype(jnp.float32)
    grad_rows = lax.all_gather(down_grad, "tensor", axis=0, tiled=True)
    layer_out = (residual + branch).reshape(blocks, half_len, model_width).astype(jnp.bfloat16)
    hidden_grad = contract_last(grad_rows, down_all)
    gate_grad = (
        hidden_grad * up_pre * sigmoid_gate * (1.0 + gate_pre * (1.0 - sigmoid_gate))
    ).astype(jnp.bfloat16)
    up_grad = (hidden_grad * silu_gate).astype(jnp.bfloat16)
    grad_down = contract_rows(hidden, grad_rows)
    grad_gate = contract_rows(ffn_in, gate_grad)
    grad_up = contract_rows(ffn_in, up_grad)
    normed_grad_two = lax.psum_scatter(
        (contract_last(gate_grad, gate_all) + contract_last(up_grad, up_all)).astype(jnp.bfloat16),
        "tensor",
        scatter_dimension=0,
        tiled=True,
    ).astype(jnp.float32)
    grad_gate, grad_up, grad_down = (
        lax.psum_scatter(grad_gate, ("fsdp", "heads"), scatter_dimension=0, tiled=True),
        lax.psum_scatter(grad_up, ("fsdp", "heads"), scatter_dimension=0, tiled=True),
        lax.psum_scatter(grad_down, ("fsdp", "heads"), scatter_dimension=1, tiled=True),
    )
    gain_two_part = jnp.sum(normed_grad_two * residual * scale_two, axis=0)
    residual_grad = down_grad.astype(jnp.float32) + norm_back(
        residual, scale_two, gain_two, normed_grad_two
    )
    residual_low = residual_grad.astype(jnp.bfloat16).reshape(blocks, half_len, model_width)
    grad_whole = lax.all_gather(residual_low, "heads", axis=1, tiled=True).reshape(
        blocks * length, model_width
    )
    attended_grad = contract_last(grad_whole, out_w).astype(jnp.bfloat16)
    grad_out = contract_rows(attended_low, grad_whole)
    grad_tiles = attended_grad.reshape(
        blocks, tile_count, tile_rows, key_heads_local, group_size, head_size
    )
    grad_tiles = grad_tiles.transpose(0, 3, 1, 4, 2, 5).reshape(
        total_tiles, group_size, tile_rows, head_size
    )

    def backward_tile(element):
        tile_index, logsum, grad_tile = element
        query_tile, key_tile, value_tile, allowed = pick(tile_index)
        return tile_backward(query_tile, key_tile, value_tile, allowed, logsum, grad_tile, factor)

    query_grads, key_grads, value_grads = lax.map(backward_tile, (tile_ids, logsums, grad_tiles))
    query_grads = query_grads.reshape(
        blocks, key_heads_local, tile_count, group_size, tile_rows, head_size
    )
    query_grads = query_grads.transpose(0, 2, 4, 1, 3, 5).reshape(
        blocks, length, query_heads_local, head_size
    )
    key_grads = (
        key_grads.reshape(blocks, key_heads_local, tile_count, length, head_size)
        .sum(axis=2)
        .transpose(0, 2, 1, 3)
    )
    value_grads = (
        value_grads.reshape(blocks, key_heads_local, tile_count, length, head_size)
        .sum(axis=2)
        .transpose(0, 2, 1, 3)
    )
    query_raw_grad = (
        rotate_back(query_grads, cosine, sines)
        .astype(jnp.bfloat16)
        .reshape(blocks * length, query_heads_local * head_size)
    )
    key_raw_grad = (
        rotate_back(key_grads, cosine, sines)
        .astype(jnp.bfloat16)
        .reshape(blocks * length, key_heads_local * head_size)
    )
    value_grad = value_grads.astype(jnp.bfloat16).reshape(
        blocks * length, key_heads_local * head_size
    )
    grad_query = contract_rows(normed_one, query_raw_grad)
    grad_key = contract_rows(normed_one, key_raw_grad)
    grad_value = contract_rows(normed_one, value_grad)
    normed_grad_one = (
        contract_last(query_raw_grad, query_w)
        + contract_last(key_raw_grad, key_w)
        + contract_last(value_grad, value_w)
    )
    gain_one_part = jnp.sum(normed_grad_one * rows_one * scale_one, axis=0)
    token_part = norm_back(rows_one, scale_one, gain_one, normed_grad_one).reshape(
        blocks, length, model_width
    )
    paired = jnp.stack([gain_one_part, gain_two_part])
    repeated = jnp.broadcast_to(paired[None], (head_count, 2, model_width))
    token_sum, gain_sum = (
        lax.psum_scatter(
            token_part.astype(jnp.bfloat16), "heads", scatter_dimension=1, tiled=True
        ).astype(jnp.float32),
        lax.psum_scatter(
            repeated.astype(jnp.bfloat16), "heads", scatter_dimension=0, tiled=True
        ).astype(jnp.float32),
    )
    grad_tokens = residual_grad.reshape(blocks, half_len, model_width) + token_sum
    grad_query, grad_key, grad_value, grad_out, grad_norm_first, grad_norm_second = (
        lax.psum_scatter(grad_query, ("fsdp", "tensor"), scatter_dimension=0, tiled=True),
        lax.psum_scatter(grad_key, ("fsdp", "tensor"), scatter_dimension=0, tiled=True),
        lax.psum_scatter(grad_value, ("fsdp", "tensor"), scatter_dimension=0, tiled=True),
        lax.psum_scatter(grad_out, ("fsdp", "tensor"), scatter_dimension=1, tiled=True),
        lax.psum_scatter(gain_sum[0, 0], ("fsdp", "tensor"), scatter_dimension=0, tiled=True),
        lax.psum_scatter(gain_sum[0, 1], ("fsdp", "tensor"), scatter_dimension=0, tiled=True),
    )
    return (
        layer_out,
        grad_tokens,
        grad_query,
        grad_key,
        grad_value,
        grad_out,
        grad_norm_first,
        grad_norm_second,
        grad_gate,
        grad_up,
        grad_down,
    )


def solution(mesh):
    placed = (
        P(("fsdp", "tensor"), "heads", None),
        P(("fsdp", "tensor"), None),
        P(("fsdp", "tensor"), "heads", None),
        P(("fsdp", "tensor"), "heads"),
        P(("fsdp", "tensor"), "heads"),
        P(("fsdp", "tensor"), "heads"),
        P("heads", ("fsdp", "tensor")),
        P(("fsdp", "tensor")),
        P(("fsdp", "tensor")),
        P(("fsdp", "heads"), "tensor"),
        P(("fsdp", "heads"), "tensor"),
        P("tensor", ("fsdp", "heads")),
    )
    return jax.shard_map(
        local,
        mesh=mesh,
        in_specs=placed,
        out_specs=(
            P(("fsdp", "tensor"), "heads", None),
            P(("fsdp", "tensor"), "heads", None),
            P(("fsdp", "tensor"), "heads"),
            P(("fsdp", "tensor"), "heads"),
            P(("fsdp", "tensor"), "heads"),
            P("heads", ("fsdp", "tensor")),
            P(("fsdp", "tensor")),
            P(("fsdp", "tensor")),
            P(("fsdp", "heads"), "tensor"),
            P(("fsdp", "heads"), "tensor"),
            P("tensor", ("fsdp", "heads")),
        ),
        check_vma=False,
    )
```

profile of v0, /device:TPU:9, one launch (start us, length us, event | category | flops | bytes accessed | tf_op | source)
XLA Modules:
  0.0 1444.1 jit_solution(16151099589941806583)
XLA Ops:
  13.5 29.9 %all-reduce.8 = (bf16[1152]{0:T(1024)(128)(2,1)S(1)}, bf16[1152]{0:T(1024)(128)(2,1)S(1)}) all-reduce(bf16[1152]{0:T(1024)(128)(2,1)S(1)} %dynamic-update-slice, bf16[1152]{0:T(1024)(128)(2,1)S(1)} %dynamic-update-slice.1), channel_id=1, replica_groups=mesh['fsdp'=4,'heads'=2,'tensor'=4] {'fsdp','tensor'}, use_global_device_ids=true, to_apply=%add | all-reduce | flops 2304 | bytes 9216
  44.6 37.7 %all_gather.42 = bf16[1152,192]{1,0:T(8,128)(2,1)} all-gather(bf16[72,192]{1,0:T(8,128)(2,1)S(1)} %copy-done.26), channel_id=1, replica_groups=mesh['fsdp'=4,'heads'=2,'tensor'=4] {'fsdp','tensor'}, dimensions={0}, use_global_device_ids=true | all-gather | bytes 470016 | tf_op jit(solution)/shard_map/all_gather | solution.py:133
  82.3 33.6 %all_gather.43 = bf16[1152,192]{1,0:T(8,128)(2,1)} all-gather(bf16[72,192]{1,0:T(8,128)(2,1)S(1)} %copy-done.27), channel_id=1, replica_groups=mesh['fsdp'=4,'heads'=2,'tensor'=4] {'fsdp','tensor'}, dimensions={0}, use_global_device_ids=true | all-gather | bytes 470016 | tf_op jit(solution)/shard_map/all_gather | solution.py:134
  124.0 3.3 fusion.119
  128.3 68.7 %while.36 = (s32[]{:T(128)}, bf16[6,3,512,64]{2,3,1,0:T(8,128)(2,1)}, f32[6,3,512]{2,1,0:T(4,128)}, s32[6]{0:T(128)S(1)}, s32[1,1024]{1,0:T(1,128)S(1)}, /*index...) while((s32[]{:T(128)}, ...), condition=%wide.region_7.8_spmd.clone.clone, body=%wide.region_4.7_spmd.clone.sunk.clone | while | flops 423099424 | bytes 21891008 | solution.py:199
  135.5 3.8 fusion.209
  146.9 3.8 fusion.209
  158.3 3.8 fusion.209
  169.7 3.8 fusion.209
  181.1 3.8 fusion.209
  192.5 3.8 fusion.209
  196.9 3.1 copy.35
  201.3 5.4 fusion.81
  207.3 36.1 %reduce-scatter.16.cloned.1.call-done = bf16[1,512,1152]{2,1,0:T(8,128)(2,1)} async-done(((bf16[1,1024,1152]{2,1,0:T(8,128)(2,1)}), bf16[1,512,1152]{2,1,0:T(8,128)(2,1)}) %reduce-scatter.16.cloned.1.call-update) | async-done | bytes 1179664 | tf_op jit(solution)/shard_map/reduce_scatter | solution.py:210
  249.7 12.0 all-gather.22.cloned.1.call-done
  261.7 58.2 %all-gather.18.cloned.1.call-done = bf16[2048,1152]{1,0:T(8,128)(2,1)} async-done(((bf16[512,1152]{1,0:T(8,128)(2,1)}), bf16[2048,1152]{1,0:T(8,128)(2,1)}) %all-gather.18.cloned.1.call-update) | async-done | bytes 4718608 | tf_op jit(solution)/shard_map/all_gather | solution.py:219
  319.8 9.8 fusion.127
  329.6 18.8 %all-gather.20.cloned.1.call-done = bf16[1152,768]{1,0:T(8,128)(2,1)} async-done(((bf16[144,768]{1,0:T(8,128)(2,1)}), bf16[1152,768]{1,0:T(8,128)(2,1)}) %all-gather.20.cloned.1.call-update) | async-done | bytes 1769488 | tf_op jit(solution)/shard_map/all_gather | solution.py:142
  348.4 9.8 fusion.126
  358.2 17.8 %all-gather.24.cloned.1.call-done = bf16[768,1152]{0,1:T(8,128)(2,1)} async-done(((bf16[768,144]{0,1:T(8,128)(2,1)}), bf16[768,1152]{0,1:T(8,128)(2,1)}) %all-gather.24.cloned.1.call-update) | async-done | bytes 1769488 | tf_op jit(solution)/shard_map/all_gather | solution.py:144
  376.0 57.8 %all-gather.26.cloned.1.call-done = bf16[1,2048,1152]{2,1,0:T(8,128)(2,1)} async-done(((bf16[1,512,1152]{2,1,0:T(8,128)(2,1)}), bf16[1,2048,1152]{2,1,0:T(8,128)(2,1)}) %all-gather.26.cloned.1.call-update) | async-done | bytes 4718608 | tf_op jit(solution)/shard_map/all_gather | solution.py:231
  433.7 12.7 multiply_convert_fusion.1
  446.5 4.3 fusion.128
  450.8 6.0 add_convert_fusion
  456.9 8.9 convolution_convert_fusion
  466.1 47.8 %reduce-scatter.20.cloned.1.call-done = bf16[512,1152]{1,0:T(8,128)(2,1)} async-done(((bf16[2048,1152]{1,0:T(8,128)(2,1)}), bf16[512,1152]{1,0:T(8,128)(2,1)}) %reduce-scatter.20.cloned.1.call-update) | async-done | bytes 1179664 | tf_op jit(solution)/shard_map/reduce_scatter | solution.py:241
  513.9 2.9 fusion.88
  517.4 56.6 %reduce-scatter.18.cloned.1.call-done = bf16[512,1152]{1,0:T(8,128)(2,1)} async-done(((bf16[2048,1152]{1,0:T(8,128)(2,1)}), bf16[512,1152]{1,0:T(8,128)(2,1)}) %reduce-scatter.18.cloned.1.call-update) | async-done | bytes 1179664 | tf_op jit(solution)/shard_map/reduce_scatter | solution.py:225
  574.0 4.1 fusion.121
  578.2 11.9 all-gather.28.cloned.1.call-done
  590.1 4.8 convolution_convert_fusion.2
  594.9 4.0 reshape.760
  602.0 125.7 %while.37 = (s32[]{:T(128)}, f32[6,3,512,64]{2,3,1,0:T(8,128)}, f32[6,1024,64]{1,2,0:T(8,128)}, f32[6,1024,64]{1,2,0:T(8,128)}, s32[6]{0:T(128)}, /*index=5*/s32...) while((s32[]{:T(128)}, f32[6,3,512,64]{2,3,1,0:T(8,128)}, ...), condition=%wide.region_15.16_spmd.clone.clone, body=%wide.region_13.15_spmd.clone.sunk.clone | while | flops 1031961600 | bytes 51440620 | solution.py:274
  609.2 3.5 fusion.222
  612.7 3.3 multiply_reduce_fusion.3
  620.2 2.7 fusion.220
  630.1 3.5 fusion.222
  633.7 3.3 multiply_reduce_fusion.3
  651.1 3.5 fusion.222
  654.6 3.3 multiply_reduce_fusion.3
  672.0 3.5 fusion.222
  675.6 3.3 multiply_reduce_fusion.3
  693.0 3.5 fusion.222
  696.5 3.3 multiply_reduce_fusion.3
  714.0 3.5 fusion.222
  717.5 3.3 multiply_reduce_fusion.3
  724.9 2.7 fusion.220
  732.5 5.0 copy.42
  738.6 4.4 reshape.764
  761.7 8.9 fusion.77
  770.7 9.3 fusion.131
  780.1 9.4 fusion.132
  789.7 3.8 fusion.112
  793.6 3.8 fusion.110
  797.5 5.9 fusion.130
  803.5 5.9 fusion.114
  813.2 3.2 all-reduce.4
  818.4 57.7 %all-reduce.7 = (f32[1152]{0:T(1024)}, f32[1152]{0:T(1024)}) all-reduce(f32[1152]{0:T(1024)} %get-tuple-element.406, f32[1152]{0:T(1024)} %get-tuple-element.405), channel_id=13, replica_groups=mesh['fsdp'=4,'heads'=2,'tensor'=4] {'fsdp','tensor'}, use_global_device_ids=true, to_apply=%region_27.28.clone | all-reduce | flops 2304 | bytes 18432
  878.7 4.1 bitcast_add_fusion.1
  882.8 26.7 %reduce-scatter.30.cloned.1.call-done = f32[144,768]{1,0:T(8,128)} async-done(((f32[1152,768]{1,0:T(8,128)}), f32[144,768]{1,0:T(8,128)}) %reduce-scatter.30.cloned.1.call-update) | async-done | bytes 442384 | tf_op jit(solution)/shard_map/reduce_scatter | solution.py:249
  909.4 128.0 %reduce-scatter.24.cloned.1.call-done = f32[72,192]{1,0:T(8,128)} async-done(((f32[1152,192]{1,0:T(8,128)}), f32[72,192]{1,0:T(8,128)}) %reduce-scatter.24.cloned.1.call-update) | async-done | bytes 55312 | tf_op jit(solution)/shard_map/reduce_scatter | solution.py:329
  1037.4 128.7 %reduce-scatter.26.cloned.1.call-done = f32[72,192]{1,0:T(8,128)} async-done(((f32[1152,192]{1,0:T(8,128)}), f32[72,192]{1,0:T(8,128)}) %reduce-scatter.26.cloned.1.call-update) | async-done | bytes 55312 | tf_op jit(solution)/shard_map/reduce_scatter | solution.py:330
  1166.1 135.2 %reduce-scatter.36.cloned.1.call-done = f32[576,72]{0,1:T(8,128)} async-done(((f32[576,1152]{0,1:T(8,128)}), f32[576,72]{0,1:T(8,128)}) %reduce-scatter.36.cloned.1.call-update) | async-done | bytes 165904
  1301.3 135.5 %reduce-scatter.34.cloned.1.call-done = f32[72,576]{1,0:T(8,128)} async-done(((f32[1152,576]{1,0:T(8,128)}), f32[72,576]{1,0:T(8,128)}) %reduce-scatter.34.cloned.1.call-update) | async-done | bytes 165904
  (276 shorter events, 153.1 us)
Async XLA Ops:
  8.0 3.7 copy-start.30
  8.0 3.5 copy-start.31
  8.0 4.9 copy-start.35
  8.0 5.2 copy-start.36
  8.1 36.5 %copy-start.26 = (bf16[72,192]{1,0:T(8,128)(2,1)S(1)}, bf16[72,192]{1,0:T(8,128)(2,1)}, u32[]{:S(2)}) copy-start(bf16[72,192]{1,0:T(8,128)(2,1)} %param.20) | copy-start | bytes 82948
  8.1 74.2 %copy-start.27 = (bf16[72,192]{1,0:T(8,128)(2,1)S(1)}, bf16[72,192]{1,0:T(8,128)(2,1)}, u32[]{:S(2)}) copy-start(bf16[72,192]{1,0:T(8,128)(2,1)} %param.21) | copy-start | bytes 82948
  8.1 107.8 %all-gather.12.cloned.1.call-start = ((), (), s32[]{:S(2)}) async-start(), calls=%async_computation.11 | async-start | bytes 3538944 | tf_op jit(solution)/shard_map/all_gather | solution.py:146
  8.8 115.2 %all-gather.14.cloned.1.call-start = ((), (), s32[]{:S(2)}) async-start(), calls=%async_computation.12 | async-start | bytes 1566720 | tf_op jit(solution)/shard_map/all_gather | solution.py:132
  9.6 191.7 %all-gather.16.cloned.1.call-start = ((), (), s32[]{:S(2)}) async-start(), calls=%async_computation.13 | async-start | bytes 1566720 | tf_op jit(solution)/shard_map/all_gather | solution.py:135
  10.3 233.1 %reduce-scatter.16.cloned.1.call-start = ((), (), s32[]{:S(2)}) async-start(), calls=%async_computation.14 | async-start | bytes 3538944 | tf_op jit(solution)/shard_map/reduce_scatter | solution.py:210
  43.4 80.6 %copy-start.22 = (f32[1152]{0:T(1024)}, f32[1152]{0:T(1024)S(1)}, u32[]{:S(2)}) copy-start(f32[1152]{0:T(1024)S(1)} %convert_element_type.204) | copy-start | bytes 13828
  44.6 83.0 %copy-start.7 = (f32[1024,64]{0,1:T(8,128)}, f32[1024,64]{0,1:T(8,128)S(1)}, u32[]{:S(2)}) copy-start(f32[1024,64]{0,1:T(8,128)S(1)} %get-tuple-element.472) | copy-start | bytes 786436
  44.6 83.0 %copy-start.13 = (f32[1024,64]{0,1:T(8,128)}, f32[1024,64]{0,1:T(8,128)S(1)}, u32[]{:S(2)}) copy-start(f32[1024,64]{0,1:T(8,128)S(1)} %get-tuple-element.473) | copy-start | bytes 786436
  115.9 3.0 copy-start.4
  118.9 5.1 copy-start.24
  121.0 1.1 copy-start.15
  196.9 4.4 copy-start.9
  196.9 4.4 copy-start.10
  206.7 36.8 %copy-start = (bf16[1,512,1152]{2,1,0:T(8,128)(2,1)S(1)}, bf16[1,512,1152]{2,1,0:T(8,128)(2,1)}, u32[]{:S(2)}) copy-start(bf16[1,512,1152]{2,1,0:T(8,128)(2,1)} %param.16) | copy-start | bytes 3538948
  206.7 55.0 %all-gather.22.cloned.1.call-start = ((), (), s32[]{:S(2)}) async-start(), calls=%async_computation.17 | async-start | bytes 1990656 | tf_op jit(solution)/shard_map/all_gather | solution.py:143
  207.3 112.6 %all-gather.18.cloned.1.call-start = ((), (), s32[]{:S(2)}) async-start(), calls=%async_computation.15 | async-start | bytes 5898240 | tf_op jit(solution)/shard_map/all_gather | solution.py:219
  243.4 2.4 copy-start.1
  247.4 101.1 %all-gather.20.cloned.1.call-start = ((), (), s32[]{:S(2)}) async-start(), calls=%async_computation.16 | async-start | bytes 1990656 | tf_op jit(solution)/shard_map/all_gather | solution.py:142
  247.9 128.1 %all-gather.24.cloned.1.call-start = ((), (), s32[]{:S(2)}) async-start(), calls=%async_computation.18 | async-start | bytes 1990656 | tf_op jit(solution)/shard_map/all_gather | solution.py:144
  248.7 185.1 %all-gather.26.cloned.1.call-start = ((), (), s32[]{:S(2)}) async-start(), calls=%async_computation.27 | async-start | bytes 5898240 | tf_op jit(solution)/shard_map/all_gather | solution.py:231
  249.4 264.5 %reduce-scatter.20.cloned.1.call-start = ((), (), s32[]{:S(2)}) async-start(), calls=%async_computation.20 | async-start | bytes 5898240 | tf_op jit(solution)/shard_map/reduce_scatter | solution.py:241
  433.7 12.7 copy-start.33
  446.5 4.3 copy-start.38
  446.5 4.3 copy-start.37
  446.5 4.3 copy-start.32
  456.9 117.1 %reduce-scatter.18.cloned.1.call-start = ((), (), s32[]{:S(2)}) async-start(), calls=%async_computation.19 | async-start | bytes 5898240 | tf_op jit(solution)/shard_map/reduce_scatter | solution.py:225
  465.9 124.2 %all-gather.28.cloned.1.call-start = ((), (), s32[]{:S(2)}) async-start(), calls=%async_computation.28 | async-start | bytes 3538944 | tf_op jit(solution)/shard_map/all_gather | solution.py:257
  513.9 60.1 %copy-start.6 = (bf16[512,1152]{1,0:T(8,128)(2,1)S(1)}, bf16[512,1152]{1,0:T(8,128)(2,1)}, u32[]{:S(2)}) copy-start(bf16[512,1152]{1,0:T(8,128)(2,1)} %reduce-scatter.20.cloned.1.call-done) | copy-start | bytes 3538948
  578.2 300.5 %reduce-scatter.22.cloned.1.call-start = ((), (), s32[]{:S(2)}) async-start(), calls=%async_computation.21 | async-start | bytes 3538944 | tf_op jit(solution)/shard_map/reduce_scatter | solution.py:319
  732.5 5.0 copy-start.11
  732.5 5.0 copy-start.14
  744.9 1.7 copy-start.2
  746.6 0.9 copy-start.8
  746.6 1.2 copy-start.12
  746.6 1.3 copy-start.20
  746.6 1.4 copy-start.21
  746.6 2.2 copy-start.3
  748.2 6.2 copy-start.19
  750.7 1.4 copy-start.34
  752.1 2.3 copy-start.17
  754.3 1.7 copy-start.5
  754.4 1.8 copy-start.16
  754.4 1.9 copy-start.18
  754.4 1.9 copy-start.23
  754.4 1.8 copy-start.25
  756.2 2.7 copy-start.29
  761.2 121.5 %reduce-scatter.32.cloned.1.call-start = ((), (), s32[]{:S(2)}) async-start(), calls=%async_computation.26 | async-start | bytes 3981312 | tf_op jit(solution)/shard_map/reduce_scatter | solution.py:250
  770.6 112.1 %reduce-scatter.28.cloned.1.call-start = ((), (), s32[]{:S(2)}) async-start(), calls=%async_computation.24 | async-start | bytes 3981312 | tf_op jit(solution)/shard_map/reduce_scatter | solution.py:248
  780.0 129.4 %reduce-scatter.30.cloned.1.call-start = ((), (), s32[]{:S(2)}) async-start(), calls=%async_computation.25 | async-start | bytes 3981312 | tf_op jit(solution)/shard_map/reduce_scatter | solution.py:249
  789.5 247.9 %reduce-scatter.24.cloned.1.call-start = ((), (), s32[]{:S(2)}) async-start(), calls=%async_computation.22 | async-start | bytes 1253376 | tf_op jit(solution)/shard_map/reduce_scatter | solution.py:329
  793.6 372.5 %reduce-scatter.26.cloned.1.call-start = ((), (), s32[]{:S(2)}) async-start(), calls=%async_computation.23 | async-start | bytes 1253376 | tf_op jit(solution)/shard_map/reduce_scatter | solution.py:330
  797.5 503.8 %reduce-scatter.36.cloned.1.call-start = ((), (), s32[]{:S(2)}) async-start(), calls=%async_computation.30 | async-start | bytes 3133440
  803.4 633.4 %reduce-scatter.34.cloned.1.call-start = ((), (), s32[]{:S(2)}) async-start(), calls=%async_computation.29 | async-start | bytes 3133440
  809.4 69.3 %copy-start.28 = (f32[512]{0:T(512)S(1)}, f32[512]{0:T(512)}, u32[]{:S(2)}) copy-start(f32[512]{0:T(512)} %get-tuple-element.476) | copy-start | bytes 6148
Sparse Core Ops, SparseCore 0:
  10.5 12.8 all-gather.11
  26.0 58.7 all-gather.13
  87.6 57.9 all-gather.15
  206.8 36.5 reduce-scatter.15
  578.3 11.7 all-gather.27
  761.4 11.0 reduce-scatter.21
  775.4 42.7 reduce-scatter.31
  821.2 43.2 reduce-scatter.27
  867.4 41.9 reduce-scatter.29
  915.3 122.0 reduce-scatter.23
  1043.5 122.5 reduce-scatter.25
  1172.3 128.9 reduce-scatter.35
  1307.7 129.0 reduce-scatter.33
Sparse Core Ops, SparseCore 1:
  208.8 52.8 all-gather.21
  264.1 55.7 all-gather.17
  321.4 26.9 all-gather.19
  350.2 25.7 all-gather.23
  378.0 55.7 all-gather.25
  456.9 56.9 reduce-scatter.19
  517.0 56.9 reduce-scatter.17
where the time goes:
time: 1460 us; the launch traced here: 1440 us
  waiting for transfers between devices  876 us (60%)
  matrix products  236 us (16%)
  blocking collectives  162 us (11%)
  other arithmetic  69.2 us (5%)
  local copies, waits for them, and re-layouts  49.9 us (3%)
  loops' own time  31.9 us (2%)
  between operations  17.4 us (1%)
    unnamed x22, waiting for transfers between devices  275 us
    reduce_scatter x1, waiting for transfers between devices, local(): lax.psum_scatter(grad_value, ('fsdp', 'tensor'), scatter_dimension=0, til...  129 us
    reduce_scatter x1, waiting for transfers between devices, local(): lax.psum_scatter(grad_key, ('fsdp', 'tensor'), scatter_dimension=0, tiled...  128 us
    unnamed x3, blocking collectives  90.8 us
    all_gather x1, waiting for transfers between devices, local(): ffn_in = lax.all_gather(normed_two, 'tensor', axis=0, tiled=True)  58.2 us
    all_gather x1, waiting for transfers between devices, local(): grad_rows = lax.all_gather(down_grad, 'tensor', axis=0, tiled=True)  57.8 us
    reduce_scatter x1, waiting for transfers between devices, local(): lax.psum_scatter(jnp.dot(hidden, down_all, preferred_element_type=jnp.flo...  56.6 us
    reduce_scatter x1, waiting for transfers between devices, local(): lax.psum_scatter((contract_last(gate_grad, gate_all) + contract_last(up_g...  47.8 us
  transfers between devices with their start and end apart: 20, of which 14 were waited for; matrix products, arithmetic and copies ran while one was open for 12% of the time, Pallas kernels for 0%

commit v1 on v0

v1 whole, which is shorter than its diff:
```python
import jax
import jax.numpy as jnp
from jax import lax
from jax.experimental import pallas as pl
from jax.experimental.pallas import tpu as pltpu
from jax.sharding import PartitionSpec as P

HQ = 18
KVH = 6
HD = 64


epsilon = 1e-05
theta_base = 10000.0
mask_fill = -1e30


def contract_rows(left_side, right_side):
    return lax.dot_general(
        left_side, right_side, (((0,), (0,)), ((), ())), preferred_element_type=jnp.float32
    )


def contract_last(left_side, right_side):
    return lax.dot_general(
        left_side, right_side, (((1,), (1,)), ((), ())), preferred_element_type=jnp.float32
    )


def rms_scale(values):
    return lax.rsqrt(jnp.mean(values * values, axis=-1, keepdims=True) + epsilon)


def norm_back(values, inverse_rms, gains, upstream):
    weighted = gains * upstream
    cubed = inverse_rms * inverse_rms * inverse_rms
    return inverse_rms * weighted - values * cubed * jnp.mean(
        values * weighted, axis=-1, keepdims=True
    )


def positions(seq_lens, length):
    ending = jnp.cumsum(seq_lens, axis=1)
    places = jnp.arange(length, dtype=jnp.int32)
    passed = places[None, :, None] >= ending[:, None, :]
    segment = jnp.sum(passed.astype(jnp.int32), axis=2)
    starts = jnp.sum(jnp.where(passed, seq_lens[:, None, :], 0), axis=2)
    return (segment, places[None, :] - starts)


def rotary(offset, head_size):
    half_size = head_size // 2
    frequency = theta_base ** (-2.0 * jnp.arange(half_size, dtype=jnp.float32) / head_size)
    angles = offset.astype(jnp.float32)[..., None] * frequency
    angles = jnp.concatenate([angles, angles], axis=-1)[:, :, None, :]
    return (jnp.cos(angles), jnp.sin(angles))


def rotate(values, cosine, sines):
    half_size = values.shape[-1] // 2
    rotated = jnp.concatenate([-values[..., half_size:], values[..., :half_size]], axis=-1)
    return values * cosine + rotated * sines


def rotate_back(upstream, cosine, sines):
    half_size = upstream.shape[-1] // 2
    scaled = upstream * sines
    return upstream * cosine + jnp.concatenate(
        [scaled[..., half_size:], -scaled[..., :half_size]], axis=-1
    )


def dot_last(left_side, right_side):
    return lax.dot_general(
        left_side, right_side, (((1,), (1,)), ((), ())), preferred_element_type=jnp.float32
    )


def shifted(value, axis, step):
    size = lax.axis_size(axis)
    return lax.ppermute(value, axis, [(i, (i + step) % size) for i in range(size)])


def gather_parts(value, axis):
    return [value] + [shifted(value, axis, step) for step in range(1, lax.axis_size(axis))]


def gather_at(value, axis, place):
    size = lax.axis_size(axis)
    me = lax.axis_index(axis)
    shape = value.shape[:place] + (size,) + value.shape[place:]
    whole = jnp.zeros(shape, value.dtype)
    for step, part in enumerate(gather_parts(value, axis)):
        whole = lax.dynamic_update_slice_in_dim(
            whole, jnp.expand_dims(part, place), (me + size - step) % size, place
        )
    return whole


def scatter_at(value, axis, place):
    size = lax.axis_size(axis)
    me = lax.axis_index(axis)

    def piece(step):
        at = (me + step) % size
        return lax.squeeze(lax.dynamic_slice_in_dim(value, at, 1, place), (place,))

    total = piece(0).astype(jnp.float32)
    for step in range(1, size):
        sent = shifted(piece(step).astype(jnp.bfloat16), axis, step)
        total = total + sent.astype(jnp.float32)
    return total


def gather_two(value, first, second):
    own, width = value.shape
    major = gather_at(value, first, 0)
    both = gather_at(major, second, 1)
    return both.reshape(-1, width)


def scatter_two(value, major, minor):
    rows, width = value.shape
    many, few = lax.axis_size(major), lax.axis_size(minor)
    split = value.reshape(many, few, rows // (many * few), width)
    return scatter_at(scatter_at(split, minor, 1), major, 0)


TILE = 256


def probabilities(query, key, start, first):
    scores = dot_last(query, key)
    rows = lax.broadcasted_iota(jnp.int32, scores.shape, 0) + first
    columns = lax.broadcasted_iota(jnp.int32, scores.shape, 1)
    scores = jnp.where((columns >= start) & (columns <= rows), scores, mask_fill)
    largest = jnp.max(scores, axis=-1, keepdims=True)
    raised = jnp.exp(scores - largest)
    return raised * (1.0 / jnp.sum(raised, axis=-1, keepdims=True))


def attention_kernel(start_ref, query_ref, key_ref, value_ref, out_ref):
    length = query_ref.shape[1]
    tile = min(TILE, length)
    for first in range(0, length, tile):
        last = first + tile
        query = query_ref[0, first:last, :] * jnp.bfloat16(HD**-0.5)
        chances = probabilities(query, key_ref[0, :last, :], start_ref[first:last, :], first)
        out_ref[0, first:last, :] = jnp.dot(
            chances.astype(jnp.bfloat16), value_ref[0, :last, :], preferred_element_type=jnp.float32
        ).astype(jnp.bfloat16)


def attention_back_kernel(
    start_ref, query_ref, key_ref, value_ref, grad_ref, query_grad_ref, key_grad_ref, value_grad_ref
):
    length = query_ref.shape[1]
    tile = min(TILE, length)
    group = HQ // KVH

    @pl.when(pl.program_id(0) % group == 0)
    def _():
        key_grad_ref[...] = jnp.zeros_like(key_grad_ref)
        value_grad_ref[...] = jnp.zeros_like(value_grad_ref)

    for first in range(0, length, tile):
        last = first + tile
        query = query_ref[0, first:last, :] * jnp.bfloat16(HD**-0.5)
        key = key_ref[0, :last, :]
        grad = grad_ref[0, first:last, :]
        chances = probabilities(query, key, start_ref[first:last, :], first)
        chance_grad = dot_last(grad, value_ref[0, :last, :])
        centre = jnp.sum(chances * chance_grad, axis=-1, keepdims=True)
        score_grad = (chances * (chance_grad - centre)).astype(jnp.bfloat16)
        query_grad_ref[0, first:last, :] = jnp.dot(
            score_grad, key, preferred_element_type=jnp.float32
        ) * (HD**-0.5)
        key_grad_ref[0, :last, :] += contract_rows(score_grad, query)
        value_grad_ref[0, :last, :] += contract_rows(chances.astype(jnp.bfloat16), grad)


def attention_specs(length):
    group = HQ // KVH
    start = pl.BlockSpec((length, 1), lambda h: (0, 0))
    query = pl.BlockSpec((1, length, HD), lambda h: (h, 0, 0))
    key = pl.BlockSpec((1, length, HD), lambda h: (h // group, 0, 0))
    return start, query, key


def attention(start, queries, keys, values):
    heads, length, _ = queries.shape
    at_start, at_query, at_key = attention_specs(length)
    pairs = heads * length * length
    return pl.pallas_call(
        attention_kernel,
        grid=(heads,),
        in_specs=[at_start, at_query, at_key, at_key],
        out_specs=at_query,
        out_shape=jax.ShapeDtypeStruct(queries.shape, jnp.bfloat16),
        cost_estimate=pl.CostEstimate(
            flops=30 * pairs * 8, bytes_accessed=heads * length * HD * 8, transcendentals=pairs
        ),
        compiler_params=pltpu.CompilerParams(vmem_limit_bytes=40 * 1024 * 1024),
        name="attention",
    )(start, queries, keys, values)


def attention_back(start, queries, keys, values, grads):
    heads, length, _ = queries.shape
    at_start, at_query, at_key = attention_specs(length)
    pairs = heads * length * length
    return pl.pallas_call(
        attention_back_kernel,
        grid=(heads,),
        in_specs=[at_start, at_query, at_key, at_key, at_query],
        out_specs=[at_query, at_key, at_key],
        out_shape=[
            jax.ShapeDtypeStruct(queries.shape, jnp.float32),
            jax.ShapeDtypeStruct(keys.shape, jnp.float32),
            jax.ShapeDtypeStruct(keys.shape, jnp.float32),
        ],
        cost_estimate=pl.CostEstimate(
            flops=60 * pairs * 16, bytes_accessed=heads * length * HD * 16, transcendentals=pairs
        ),
        compiler_params=pltpu.CompilerParams(vmem_limit_bytes=40 * 1024 * 1024),
        name="attention_back",
    )(start, queries, keys, values, grads)


def local(
    tokens,
    seq_lens,
    cotangent,
    w_query,
    w_key,
    w_value,
    w_out,
    norm_first,
    norm_second,
    w_gate,
    w_up,
    w_down,
):
    blocks, half_len, model_width = tokens.shape
    head_count = lax.axis_size("heads")
    tensor_count = lax.axis_size("tensor")
    length = half_len * head_count
    rows = blocks * length
    heads = w_query.shape[1] // HD
    kv_heads = w_key.shape[1] // HD
    query_width = heads * HD
    key_width = kv_heads * HD
    qkv_width = query_width + 2 * key_width
    inner = w_gate.shape[1]

    own_qkv = jnp.concatenate(
        [w_query, w_key, w_value, norm_first[:, None], norm_second[:, None]], axis=1
    )
    qkv_all = gather_two(own_qkv, "fsdp", "tensor")
    out_t = gather_two(w_out.T, "fsdp", "tensor")
    qkv_w = qkv_all[:, :qkv_width]
    gain_one = qkv_all[:, qkv_width].astype(jnp.float32)
    gain_two = qkv_all[:, qkv_width + 1].astype(jnp.float32)

    rows_one = gather_at(tokens, "heads", 1).reshape(rows, model_width).astype(jnp.float32)
    scale_one = rms_scale(rows_one)
    normed_one = (rows_one * scale_one * gain_one).astype(jnp.bfloat16)
    projected = jnp.dot(normed_one, qkv_w, preferred_element_type=jnp.float32)

    down_grad = cotangent.reshape(blocks * half_len, model_width)
    ffn_own = jnp.concatenate([w_gate, w_up, w_down.T], axis=1)
    projected, down_grad, ffn_own = lax.optimization_barrier((projected, down_grad, ffn_own))
    ffn_w = gather_two(ffn_own, "fsdp", "heads")
    gate_up_w = ffn_w[:, : 2 * inner]
    down_t = ffn_w[:, 2 * inner :]
    grad_parts = gather_parts(down_grad, "tensor")

    segment, offset = positions(seq_lens, length)
    cosine, sines = rotary(offset, HD)
    starts = jnp.arange(length, dtype=jnp.int32)[None, :] - offset

    def to_heads(value, count):
        return value.reshape(blocks, length, count, HD)

    def lead(value):
        return value.transpose(0, 2, 1, 3)

    queries = lead(
        rotate(to_heads(projected[:, :query_width], heads), cosine, sines).astype(jnp.bfloat16)
    )
    keys = lead(
        rotate(
            to_heads(projected[:, query_width : query_width + key_width], kv_heads), cosine, sines
        ).astype(jnp.bfloat16)
    )
    values = lead(
        to_heads(projected[:, query_width + key_width :].astype(jnp.bfloat16), kv_heads)
    )
    attended = jnp.stack(
        [
            attention(starts[b][:, None], queries[b], keys[b], values[b])
            for b in range(blocks)
        ]
    )
    attended_low = attended.transpose(0, 2, 1, 3).reshape(rows, query_width)
    attn_part = dot_last(attended_low, out_t).astype(jnp.bfloat16)
    mixed = scatter_at(
        attn_part.reshape(blocks, head_count, half_len, model_width), "heads", 1
    )
    residual = (tokens.astype(jnp.float32) + mixed).reshape(blocks * half_len, model_width)
    scale_two = rms_scale(residual)
    normed_two = (residual * scale_two * gain_two).astype(jnp.bfloat16)

    ffn_parts = gather_parts(normed_two, "tensor")
    hiddens, gate_ups, grads_back = [], [], []
    for step in range(tensor_count):
        pre = jnp.dot(ffn_parts[step], gate_up_w, preferred_element_type=jnp.float32)
        gate_pre, up_pre = pre[:, :inner], pre[:, inner:]
        sigmoid_gate = jax.nn.sigmoid(gate_pre)
        silu_gate = gate_pre * sigmoid_gate
        hidden_grad = jnp.dot(grad_parts[step], down_t, preferred_element_type=jnp.float32)
        hiddens.append((silu_gate * up_pre).astype(jnp.bfloat16))
        gate_grad = (
            hidden_grad * up_pre * sigmoid_gate * (1.0 + gate_pre * (1.0 - sigmoid_gate))
        ).astype(jnp.bfloat16)
        up_grad = (hidden_grad * silu_gate).astype(jnp.bfloat16)
        gate_ups.append(jnp.concatenate([gate_grad, up_grad], axis=1))
        part = dot_last(gate_ups[step], gate_up_w)
        grads_back.append(
            part if step == 0 else shifted(part.astype(jnp.bfloat16), "tensor", -step)
        )
    normed_grad_two = grads_back[0]
    for part in grads_back[1:]:
        normed_grad_two = normed_grad_two + part.astype(jnp.float32)

    gain_two_part = jnp.sum(normed_grad_two * residual * scale_two, axis=0)
    residual_grad = down_grad.astype(jnp.float32) + norm_back(
        residual, scale_two, gain_two, normed_grad_two
    )
    residual_low = residual_grad.astype(jnp.bfloat16).reshape(blocks, half_len, model_width)
    grad_whole = gather_at(residual_low, "heads", 1).reshape(rows, model_width)

    hiddens[0], grad_whole = lax.optimization_barrier((hiddens[0], grad_whole))
    branch = jnp.zeros((), jnp.float32)
    for step in range(tensor_count):
        part = dot_last(hiddens[step], down_t)
        if step > 0:
            part = shifted(part.astype(jnp.bfloat16), "tensor", -step).astype(jnp.float32)
        branch = branch + part
    layer_out = (residual + branch).reshape(blocks, half_len, model_width).astype(jnp.bfloat16)
    grad_gate_up = contract_rows(jnp.concatenate(ffn_parts), jnp.concatenate(gate_ups))
    grad_down_t = contract_rows(jnp.concatenate(grad_parts), jnp.concatenate(hiddens))
    own_gate_up = scatter_two(grad_gate_up.astype(jnp.bfloat16), "fsdp", "heads")
    own_down = scatter_two(grad_down_t.astype(jnp.bfloat16), "fsdp", "heads")

    attended_grad = jnp.dot(grad_whole, out_t, preferred_element_type=jnp.float32)
    grad_out_t = contract_rows(grad_whole, attended_low)
    own_out = scatter_two(grad_out_t.astype(jnp.bfloat16), "fsdp", "tensor")
    grads = lead(to_heads(attended_grad.astype(jnp.bfloat16), heads))
    backs = [
        attention_back(starts[b][:, None], queries[b], keys[b], values[b], grads[b])
        for b in range(blocks)
    ]
    query_grads, key_grads, value_grads = (
        jnp.stack([back[at] for back in backs]).transpose(0, 2, 1, 3) for at in range(3)
    )
    raw_grad = jnp.concatenate(
        [
            rotate_back(query_grads, cosine, sines).astype(jnp.bfloat16).reshape(rows, query_width),
            rotate_back(key_grads, cosine, sines).astype(jnp.bfloat16).reshape(rows, key_width),
            value_grads.astype(jnp.bfloat16).reshape(rows, key_width),
        ],
        axis=1,
    )
    normed_grad_one = dot_last(raw_grad, qkv_w)
    grad_qkv = contract_rows(normed_one, raw_grad)
    gain_one_part = jnp.sum(normed_grad_one * rows_one * scale_one, axis=0)
    token_part = norm_back(rows_one, scale_one, gain_one, normed_grad_one)
    token_sum = scatter_at(
        token_part.astype(jnp.bfloat16).reshape(blocks, head_count, half_len, model_width),
        "heads",
        1,
    )
    grad_tokens = residual_grad.reshape(blocks, half_len, model_width) + token_sum
    own_qkv_grad = scatter_two(grad_qkv.astype(jnp.bfloat16), "fsdp", "tensor")
    gains = jnp.stack([gain_one_part, gain_two_part], axis=1)
    gains = gains + sum(shifted(gains, "heads", step) for step in range(1, head_count))
    own_gains = scatter_two(gains, "fsdp", "tensor")
    return (
        layer_out,
        grad_tokens,
        own_qkv_grad[:, :query_width],
        own_qkv_grad[:, query_width : query_width + key_width],
        own_qkv_grad[:, query_width + key_width :],
        own_out.T,
        own_gains[:, 0],
        own_gains[:, 1],
        own_gate_up[:, :inner],
        own_gate_up[:, inner:],
        own_down.T,
    )


def solution(mesh):
    placed = (
        P(("fsdp", "tensor"), "heads", None),
        P(("fsdp", "tensor"), None),
        P(("fsdp", "tensor"), "heads", None),
        P(("fsdp", "tensor"), "heads"),
        P(("fsdp", "tensor"), "heads"),
        P(("fsdp", "tensor"), "heads"),
        P("heads", ("fsdp", "tensor")),
        P(("fsdp", "tensor")),
        P(("fsdp", "tensor")),
        P(("fsdp", "heads"), "tensor"),
        P(("fsdp", "heads"), "tensor"),
        P("tensor", ("fsdp", "heads")),
    )
    return jax.shard_map(
        local,
        mesh=mesh,
        in_specs=placed,
        out_specs=(
            P(("fsdp", "tensor"), "heads", None),
            P(("fsdp", "tensor"), "heads", None),
            P(("fsdp", "tensor"), "heads"),
            P(("fsdp", "tensor"), "heads"),
            P(("fsdp", "tensor"), "heads"),
            P("heads", ("fsdp", "tensor")),
            P(("fsdp", "tensor")),
            P(("fsdp", "tensor")),
            P(("fsdp", "heads"), "tensor"),
            P(("fsdp", "heads"), "tensor"),
            P("tensor", ("fsdp", "heads")),
        ),
        check_vma=False,
    )
```

time: 1460 us -> 580 us (0.40)
  waiting for transfers between devices: 876 us -> 207 us
  blocking collectives: 162 us -> 0 us
  matrix products: 236 us -> 92.3 us
  starting transfers between devices: 1.78 us -> 74.7 us
  Pallas kernels: 0 us -> 53.1 us
  local copies, waits for them, and re-layouts: 49.9 us -> 83.9 us
  loops' own time: 31.9 us -> 0 us
  between operations: 17.4 us -> 2.13 us
    reduce_scatter x9 -> x0, waiting for transfers between devices: 424 us -> none  [the longest x1 129 us: local(): lax.psum_scatter(grad_value, ('fsdp', 'tensor'), scatter_dimension=0, til...]
    unnamed x22 -> x0, waiting for transfers between devices: 275 us -> none
    ppermute x0 -> x59, waiting for transfers between devices: none -> 207 us  [shifted(): lax.ppermute(value, axis, [(i, (i + step) % size) for i in range(size)])]
    all_gather x9 -> x0, waiting for transfers between devices: 176 us -> none  [the longest x1 58.2 us: local(): ffn_in = lax.all_gather(normed_two, 'tensor', axis=0, tiled=True)]
    dot_general x56 -> x20, matrix products: 189 us -> 65.8 us  [the longest x10 40.3 us: dot_last(): lax.dot_general(left_side, right_side, (((1,), (1,)), ((), ())), preferre...]
    unnamed x3 -> x0, blocking collectives: 90.8 us -> none
    ppermute x0 -> x59, starting transfers between devices: none -> 74.7 us  [shifted(): lax.ppermute(value, axis, [(i, (i + step) % size) for i in range(size)])]
    all_gather x2 -> x0, blocking collectives: 71.3 us -> none  [the longest x1 37.7 us: local(): lax.all_gather(w_key, ('fsdp', 'tensor'), axis=0, tiled=True)]
  transfers between devices with their start and end apart: 20 -> 59, of which waited for: 14 -> 24; matrix products, arithmetic and copies ran while one was open for 12% -> 37% of each run, Pallas kernels for 0% -> 9%
where the time goes in v1:
time: 580 us; the launch traced here: 572 us
  waiting for transfers between devices  207 us (36%)
  matrix products  92.3 us (16%)
  local copies, waits for them, and re-layouts  83.9 us (14%)
  starting transfers between devices  74.7 us (13%)
  other arithmetic  58.6 us (10%)
  Pallas kernels  53.1 us (9%)
    ppermute x59, waiting for transfers between devices, shifted(): lax.ppermute(value, axis, [(i, (i + step) % size) for i in range(size)])  207 us
    ppermute x59, starting transfers between devices, shifted(): lax.ppermute(value, axis, [(i, (i + step) % size) for i in range(size)])  74.7 us
    dot_general x10, matrix products, dot_last(): lax.dot_general(left_side, right_side, (((1,), (1,)), ((), ())), preferre...  40.3 us
    pallas_call x1, Pallas kernels, attention_back(): pl.pallas_call(attention_back_kernel, grid=(heads,), in_specs=[at_start,...  32.3 us
    dynamic_update_slice x25, local copies, waits for them, and re-layouts, gather_at(): lax.dynamic_update_slice_in_dim(whole, jnp.expand_dims(part, place), (me...  26.6 us
    dot_general x4, matrix products, contract_rows(): lax.dot_general(left_side, right_side, (((0,), (0,)), ((), ())), preferre...  26.5 us
    pallas_call x1, Pallas kernels, attention(): pl.pallas_call(attention_kernel, grid=(heads,), in_specs=[at_start, at_qu...  20.8 us
    unnamed x165, local copies, waits for them, and re-layouts  12.5 us
  transfers between devices with their start and end apart: 59, of which 24 were waited for; matrix products, arithmetic and copies ran while one was open for 37% of the time, Pallas kernels for 9%

profile of v1, /device:TPU:9, one launch (start us, length us, event | category | flops | bytes accessed | tf_op | source)
XLA Modules:
  0.0 571.6 jit_solution(1824286110845992906)
XLA Ops:
  18.4 2.2 cosine_bitcast_fusion
  20.6 3.2 collective-permute-start.8
  26.7 2.4 collective-permute-start.9
  43.0 10.1 %collective-permute-done.11 = bf16[4,72,576]{2,1,0:T(8,128)(2,1)S(1)} collective-permute-done((bf16[4,72,576]{2,1,0:T(8,128)(2,1)}, bf16[4,72,576]{2,1,0:T(8,128)(2,1)S(1)}, u32[]{:S(2)}, u32[]{:S(2)}) %collective-permute-start.11) | collective-permute-done | bytes 331808 | tf_op jit(solution)/shard_map/ppermute | solution.py:81
  53.2 8.1 %collective-permute-done.4 = bf16[4,72,962]{2,1,0:T(8,128)(2,1)S(1)} collective-permute-done((bf16[4,72,962]{2,1,0:T(8,128)(2,1)}, bf16[4,72,962]{2,1,0:T(8,128)(2,1)S(1)}, u32[]{:S(2)}, u32[]{:S(2)}) %collective-permute-start.4) | collective-permute-done | bytes 554144 | tf_op jit(solution)/shard_map/ppermute | solution.py:81
  61.4 14.7 %collective-permute-done.5 = bf16[4,72,962]{2,1,0:T(8,128)(2,1)S(1)} collective-permute-done((bf16[4,72,962]{2,1,0:T(8,128)(2,1)}, bf16[4,72,962]{2,1,0:T(8,128)(2,1)S(1)}, u32[]{:S(2)}, u32[]{:S(2)}) %collective-permute-start.5) | collective-permute-done | bytes 554144 | tf_op jit(solution)/shard_map/ppermute | solution.py:81
  80.0 2.8 fusion.66
  84.0 3.1 collective-permute-start.15
  93.8 4.9 copy.154
  98.7 8.8 %slice_negate_fusion.1 = (f32[1,1024,9,32]{3,1,2,0:T(8,128)}, f32[1,1024,9,32]{3,1,2,0:T(8,128)}) fusion(f32[1,1024,9,64]{3,1,2,0:T(8,128)} %copy.154), kind=kLoop, calls=%fused_computation.17 | loop fusion | flops 294912 | bytes 4718592 | tf_op jit(solution)/shard_map/neg | solution.py:61
  108.9 2.7 fusion.92.key_ref
  112.5 5.2 fusion.60.query_ref
  117.7 20.8 %attention.1 = bf16[9,1024,64]{2,1,0:T(8,128)(2,1)S(1)} custom-call(s32[1024,1]{1,0:T(8,128)S(1)} %copy-done.7, bf16[9,1024,64]{2,1,0:T(8,128)(2,1)S(1)} %fusion.60.query_ref, bf16[3,1024,64]{2,1,0:T(8,128)(2,1)S(1)} %fusion.92.key_ref, bf16[3,1024,64]{2,1,0:T(8,128)(2,1)S(1)} %bitcast.325), custom_call_target="tpu_custom_call" | custom-call | flops 2264924160 | bytes 4718592 | tf_op jit(solution)/shard_map/attention/pallas_call | solution.py:194
  140.6 3.9 convolution_convert_fusion.1
  156.3 2.7 collective-permute-start.18
  160.8 2.2 multiply_reduce_fusion.2
  170.8 65.3 %collective-permute-done.19 = bf16[512,1152]{1,0:T(8,128)(2,1)S(1)} collective-permute-done((bf16[512,1152]{1,0:T(8,128)(2,1)S(1)}, bf16[512,1152]{1,0:T(8,128)(2,1)S(1)}, u32[]{:S(2)}, u32[]{:S(2)}) %collective-permute-start.19) | collective-permute-done | bytes 1179680 | tf_op jit(solution)/shard_map/ppermute | solution.py:81
  237.2 2.2 fusion.102
  239.4 2.6 multiply_convert_fusion.9
  242.0 3.3 convolution_convert_fusion.9
  246.7 14.8 %collective-permute-done.22 = bf16[512,1152]{1,0:T(8,128)(2,1)S(1)} collective-permute-done((bf16[512,1152]{1,0:T(8,128)(2,1)S(1)}, bf16[512,1152]{1,0:T(8,128)(2,1)S(1)}, u32[]{:S(2)}, u32[]{:S(2)}) %collective-permute-start.22) | collective-permute-done | bytes 1179680 | tf_op jit(solution)/shard_map/ppermute | solution.py:81
  261.5 2.2 fusion.99
  263.7 2.6 multiply_convert_fusion.7
  266.3 3.3 convolution_convert_fusion.8
  270.9 2.2 fusion.105
  273.1 2.2 fusion.96
  275.4 2.6 multiply_convert_fusion.5
  278.0 3.3 convolution_convert_fusion.7
  281.4 4.4 multiply_convert_fusion.11
  285.7 13.3 %convolution_convert_fusion = bf16[1152,1536]{1,0:T(8,128)(2,1)} fusion(bf16[512,768]{1,0:T(8,128)(2,1)} %copy-done.76, bf16[512,768]{1,0:T(8,128)(2,1)} %copy-done.75, bf16[512,768]{1,0:T(8,128)(2,1)} %copy-done.74, bf16[512,768]{1,0:T(8,128)(2,1)} %copy-done.73, bf16[512,768]{1,0:T(8,128)(2,1)} %copy-done.72, bf16[512,768]{1,0:T(8,128)(2,1)} %copy-done.71, ...), kind=kOutput, calls=%fused_computation | convolution fusion | flops 7318732800 | bytes 14548992 | tf_op jit(solution)/shard_map/dot_general | solution.py:19
  301.6 3.9 convolution_convert_fusion.6
  305.4 2.6 collective-permute-start.28
  308.0 2.3 convolution_convert_fusion.5
  310.3 2.3 convolution_convert_fusion.4
  312.6 9.7 %collective-permute-done.23 = bf16[512,1152]{1,0:T(8,128)(2,1)} collective-permute-done((bf16[512,1152]{1,0:T(8,128)(2,1)}, bf16[512,1152]{1,0:T(8,128)(2,1)}, u32[]{:S(2)}, u32[]{:S(2)}) %collective-permute-start.23) | collective-permute-done | bytes 1179680 | tf_op jit(solution)/shard_map/ppermute | solution.py:81
  322.3 4.8 multiply_reduce_fusion
  334.3 9.4 %collective-permute-done.52 = bf16[144,1536]{1,0:T(8,128)(2,1)S(1)} collective-permute-done((bf16[144,1536]{1,0:T(8,128)(2,1)S(1)}, bf16[144,1536]{1,0:T(8,128)(2,1)S(1)}, u32[]{:S(2)}, u32[]{:S(2)}) %collective-permute-start.52) | collective-permute-done | bytes 442400 | tf_op jit(solution)/shard_map/ppermute | solution.py:81
  345.0 25.2 %collective-permute-done.53 = bf16[144,1536]{1,0:T(8,128)(2,1)S(1)} collective-permute-done((bf16[144,1536]{1,0:T(8,128)(2,1)S(1)}, bf16[144,1536]{1,0:T(8,128)(2,1)S(1)}, u32[]{:S(2)}, u32[]{:S(2)}) %collective-permute-start.53) | collective-permute-done | bytes 442400 | tf_op jit(solution)/shard_map/ppermute | solution.py:81
  370.4 2.6 collective-permute-done.54
  376.7 2.7 convolution_convert_fusion.3
  379.5 2.4 copy.167
  388.5 32.3 %attention_back.1 = (f32[9,1024,64]{2,1,0:T(8,128)}, f32[3,1024,64]{2,1,0:T(8,128)S(1)}, f32[3,1024,64]{2,1,0:T(8,128)S(1)}) custom-call(s32[1024,1]{1,0:T(8,128)S(1)} %copy-done.8, bf16[9,1024,64]{2,1,0:T(8,128)(2,1)S(1)} %copy-done.1, bf16[3,1024,64]{2,1,0:T(8,128)(2,1)S(1)} %copy-done.4, bf16[3,1024,64]{2,1,0:T(8,128)(2,1)S(1)} %bitcast.326, ...), custom_call_target="tpu_custom_call" | custom-call | flops 9059696640 | bytes 9437184 | tf_op jit(solution)/shard_map/attention_back/pallas_call | solution.py:212
  420.8 2.9 fusion.33
  423.7 3.8 fusion.155
  427.5 5.2 fusion.17
  432.6 4.2 copy.169
  440.4 2.2 copy.170
  443.1 8.3 %fusion.42 = (f32[1152]{0:T(1024)S(1)}, f32[1024]{0:T(1024)S(1)}, f32[1024,1152]{1,0:T(8,128)}) fusion(bf16[1,2,512,1152]{3,2,1,0:T(8,128)(2,1)} %copy-done.10, f32[1024]{0:T(1024)S(1)} %bitcast.382, f32[1152]{0:T(1024)S(1)} %copy-done.46, bf16[1152,962]{1,0:T(8,128)(2,1)} %bitcast.354, bf16[1024,192]{0,1:T(8,128)(2,1)S(1)} %bitcast.374, ...), kind=kOutput, calls=%fused_computation.54 | convolution fusion | flops 2279077888 | bytes 11277824 | tf_op jit(solution)/shard_map/dot_general | solution.py:74
  451.5 5.0 convolution_convert_fusion.2
  461.2 4.6 copy.172
  465.9 3.2 fusion.39
  472.9 5.4 fusion.43
  479.3 4.9 fusion.59
  487.4 2.2 collective-permute-start.47
  500.9 4.3 collective-permute-start.55
  505.2 5.7 collective-permute-start.31
  512.3 4.5 collective-permute-done.32
  517.1 3.3 collective-permute-done.33
  520.4 5.0 collective-permute-start.42
  525.4 3.7 collective-permute-done.34
  531.1 3.0 collective-permute-start.36
  535.0 9.5 %collective-permute-done.36 = bf16[72,960]{1,0:T(8,128)(2,1)S(1)} collective-permute-done((bf16[72,960]{1,0:T(8,128)(2,1)S(1)}, bf16[72,960]{1,0:T(8,128)(2,1)S(1)}, u32[]{:S(2)}, u32[]{:S(2)}) %collective-permute-start.36) | collective-permute-done | bytes 138272 | tf_op jit(solution)/shard_map/ppermute | solution.py:81
  552.2 12.0 %collective-permute-done.57 = bf16[144,768]{1,0:T(8,128)(2,1)S(1)} collective-permute-done((bf16[144,768]{1,0:T(8,128)(2,1)S(1)}, bf16[144,768]{1,0:T(8,128)(2,1)S(1)}, u32[]{:S(2)}, u32[]{:S(2)}) %collective-permute-start.57) | collective-permute-done | bytes 221216 | tf_op jit(solution)/shard_map/ppermute | solution.py:81
  564.2 4.6 collective-permute-done.58
  (361 shorter events, 139.7 us)
Async XLA Ops:
  3.9 29.8 %collective-permute-start.1 = (bf16[72,962]{1,0:T(8,128)(2,1)}, bf16[72,962]{1,0:T(8,128)(2,1)}, u32[]{:S(2)}, u32[]{:S(2)}) collective-permute-start(bf16[72,962]{1,0:T(8,128)(2,1)} %concatenate.64), channel_id=1, source_target_pairs={{0,8},{8,16},{16,24},{24,0},{1,9},{9,17},{17,25},{25,1},{2,10},{10... | collective-permute-start | bytes 415592 | tf_op jit(solution)/shard_map/ppermute | solution.py:81
  5.2 31.4 %collective-permute-start.2 = (bf16[72,962]{1,0:T(8,128)(2,1)}, bf16[72,962]{1,0:T(8,128)(2,1)}, u32[]{:S(2)}, u32[]{:S(2)}) collective-permute-start(bf16[72,962]{1,0:T(8,128)(2,1)} %concatenate.64), channel_id=1, source_target_pairs={{0,16},{8,24},{16,0},{24,8},{1,17},{9,25},{17,1},{25,9},{2,18},{10... | collective-permute-start | bytes 415592 | tf_op jit(solution)/shard_map/ppermute | solution.py:81
  6.2 33.1 %collective-permute-start.3 = (bf16[72,962]{1,0:T(8,128)(2,1)}, bf16[72,962]{1,0:T(8,128)(2,1)}, u32[]{:S(2)}, u32[]{:S(2)}) collective-permute-start(bf16[72,962]{1,0:T(8,128)(2,1)} %concatenate.64), channel_id=1, source_target_pairs={{0,24},{8,0},{16,8},{24,16},{1,25},{9,1},{17,9},{25,17},{2,26},{10... | collective-permute-start | bytes 415592 | tf_op jit(solution)/shard_map/ppermute | solution.py:81
  7.7 69.1 %collective-permute-start = (bf16[1,512,1152]{2,1,0:T(8,128)(2,1)}, bf16[1,512,1152]{2,1,0:T(8,128)(2,1)}, u32[]{:S(2)}, u32[]{:S(2)}) collective-permute-start(bf16[1,512,1152]{2,1,0:T(8,128)(2,1)} %param.12), channel_id=1, source_target_pairs={{0,4},{4,0},{1,5},{5,1},{2,6},{6,2},{3,7},{7,3},{8,12},{12,8},{9,1... | collective-permute-start | bytes 3538952 | tf_op jit(solution)/shard_map/ppermute | solution.py:81
  9.2 11.4 %collective-permute-start.7 = (bf16[72,576]{1,0:T(8,128)(2,1)}, bf16[72,576]{1,0:T(8,128)(2,1)}, u32[]{:S(2)}, u32[]{:S(2)}) collective-permute-start(bf16[72,576]{1,0:T(8,128)(2,1)} %bitcast.377), channel_id=1, source_target_pairs={{0,8},{8,16},{16,24},{24,0},{1,9},{9,17},{17,25},{25,1},{2,10},{10... | collective-permute-start | bytes 248840 | tf_op jit(solution)/shard_map/ppermute | solution.py:81
  20.6 91.0 %copy-start.16 = (f32[1024,64]{1,0:T(8,128)}, f32[1024,64]{1,0:T(8,128)S(1)}, u32[]{:S(2)}) copy-start(f32[1024,64]{1,0:T(8,128)S(1)} %get-tuple-element.77) | copy-start | bytes 786436
  20.6 91.0 %copy-start.19 = (f32[1024,64]{1,0:T(8,128)}, f32[1024,64]{1,0:T(8,128)S(1)}, u32[]{:S(2)}) copy-start(f32[1024,64]{1,0:T(8,128)S(1)} %get-tuple-element.78) | copy-start | bytes 786436
  20.6 6.1 %collective-permute-start.8 = (bf16[72,576]{1,0:T(8,128)(2,1)S(1)}, bf16[72,576]{1,0:T(8,128)(2,1)S(1)}, u32[]{:S(2)}, u32[]{:S(2)}) collective-permute-start(bf16[72,576]{1,0:T(8,128)(2,1)S(1)} %bitcast.378), channel_id=1, source_target_pairs={{0,16},{8,24},{16,0},{24,8},{1,17},{9,25},{17,1},{25,9},{2,18},{10... | collective-permute-start | bytes 248840 | tf_op jit(solution)/shard_map/ppermute | solution.py:81
  26.7 4.0 collective-permute-start.9
  31.4 11.3 %collective-permute-start.10 = (bf16[4,72,576]{2,1,0:T(8,128)(2,1)}, bf16[4,72,576]{2,1,0:T(8,128)(2,1)S(1)}, u32[]{:S(2)}, u32[]{:S(2)}) collective-permute-start(bf16[4,72,576]{2,1,0:T(8,128)(2,1)} %bitcast_dynamic-update-slice_fusion.23), channel_id=1, source_target_pairs={{0,1},{1,2},{2,3},{3,0},{4,5},{5,6},{6,7},{7,4},{8,9},{9,10},{10,1... | collective-permute-start | bytes 995336 | tf_op jit(solution)/shard_map/ppermute | solution.py:81
  33.7 19.3 %collective-permute-start.11 = (bf16[4,72,576]{2,1,0:T(8,128)(2,1)}, bf16[4,72,576]{2,1,0:T(8,128)(2,1)S(1)}, u32[]{:S(2)}, u32[]{:S(2)}) collective-permute-start(bf16[4,72,576]{2,1,0:T(8,128)(2,1)} %bitcast_dynamic-update-slice_fusion.23), channel_id=1, source_target_pairs={{0,2},{1,3},{2,0},{3,1},{4,6},{5,7},{6,4},{7,5},{8,10},{9,11},{10,... | collective-permute-start | bytes 995336 | tf_op jit(solution)/shard_map/ppermute | solution.py:81
  36.6 16.5 %collective-permute-start.12 = (bf16[4,72,576]{2,1,0:T(8,128)(2,1)}, bf16[4,72,576]{2,1,0:T(8,128)(2,1)S(1)}, u32[]{:S(2)}, u32[]{:S(2)}) collective-permute-start(bf16[4,72,576]{2,1,0:T(8,128)(2,1)} %bitcast_dynamic-update-slice_fusion.23), channel_id=1, source_target_pairs={{0,3},{1,0},{2,1},{3,2},{4,7},{5,4},{6,5},{7,6},{8,11},{9,8},{10,9... | collective-permute-start | bytes 995336 | tf_op jit(solution)/shard_map/ppermute | solution.py:81
  40.9 20.4 %collective-permute-start.4 = (bf16[4,72,962]{2,1,0:T(8,128)(2,1)}, bf16[4,72,962]{2,1,0:T(8,128)(2,1)S(1)}, u32[]{:S(2)}, u32[]{:S(2)}) collective-permute-start(bf16[4,72,962]{2,1,0:T(8,128)(2,1)} %bitcast_dynamic-update-slice_fusion.18), channel_id=1, source_target_pairs={{0,1},{1,2},{2,3},{3,0},{4,5},{5,6},{6,7},{7,4},{8,9},{9,10},{10,1... | collective-permute-start | bytes 1662344 | tf_op jit(solution)/shard_map/ppermute | solution.py:81
  42.7 33.5 %collective-permute-start.5 = (bf16[4,72,962]{2,1,0:T(8,128)(2,1)}, bf16[4,72,962]{2,1,0:T(8,128)(2,1)S(1)}, u32[]{:S(2)}, u32[]{:S(2)}) collective-permute-start(bf16[4,72,962]{2,1,0:T(8,128)(2,1)} %bitcast_dynamic-update-slice_fusion.18), channel_id=1, source_target_pairs={{0,2},{1,3},{2,0},{3,1},{4,6},{5,7},{6,4},{7,5},{8,10},{9,11},{10,... | collective-permute-start | bytes 1662344 | tf_op jit(solution)/shard_map/ppermute | solution.py:81
  53.1 23.1 %collective-permute-start.6 = (bf16[4,72,962]{2,1,0:T(8,128)(2,1)}, bf16[4,72,962]{2,1,0:T(8,128)(2,1)S(1)}, u32[]{:S(2)}, u32[]{:S(2)}) collective-permute-start(bf16[4,72,962]{2,1,0:T(8,128)(2,1)} %bitcast_dynamic-update-slice_fusion.18), channel_id=1, source_target_pairs={{0,3},{1,0},{2,1},{3,2},{4,7},{5,4},{6,5},{7,6},{8,11},{9,8},{10,9... | collective-permute-start | bytes 1662344 | tf_op jit(solution)/shard_map/ppermute | solution.py:81
  82.7 67.2 %collective-permute-start.14 = (bf16[144,2304]{1,0:T(8,128)(2,1)}, bf16[144,2304]{1,0:T(8,128)(2,1)}, u32[]{:S(2)}, u32[]{:S(2)}) collective-permute-start(bf16[144,2304]{1,0:T(8,128)(2,1)} %pad_maximum_fusion.3), channel_id=1, source_target_pairs={{0,8},{8,16},{16,24},{24,0},{1,9},{9,17},{17,25},{25,1},{2,10},{10... | collective-permute-start | bytes 1990664 | tf_op jit(solution)/shard_map/ppermute | solution.py:81
  84.0 68.0 %collective-permute-start.15 = (bf16[144,2304]{1,0:T(8,128)(2,1)}, bf16[144,2304]{1,0:T(8,128)(2,1)}, u32[]{:S(2)}, u32[]{:S(2)}) collective-permute-start(bf16[144,2304]{1,0:T(8,128)(2,1)} %pad_maximum_fusion.3), channel_id=1, source_target_pairs={{0,16},{8,24},{16,0},{24,8},{1,17},{9,25},{17,1},{25,9},{2,18},{10... | collective-permute-start | bytes 1990664 | tf_op jit(solution)/shard_map/ppermute | solution.py:81
  87.0 67.0 %collective-permute-start.16 = (bf16[144,2304]{1,0:T(8,128)(2,1)}, bf16[144,2304]{1,0:T(8,128)(2,1)}, u32[]{:S(2)}, u32[]{:S(2)}) collective-permute-start(bf16[144,2304]{1,0:T(8,128)(2,1)} %pad_maximum_fusion.3), channel_id=1, source_target_pairs={{0,24},{8,0},{16,8},{24,16},{1,25},{9,1},{17,9},{25,17},{2,26},{10... | collective-permute-start | bytes 1990664 | tf_op jit(solution)/shard_map/ppermute | solution.py:81
  144.7 16.1 %collective-permute-start.13 = (bf16[1,512,1152]{2,1,0:T(8,128)(2,1)S(1)}, bf16[1,512,1152]{2,1,0:T(8,128)(2,1)}, u32[]{:S(2)}, u32[]{:S(2)}) collective-permute-start(bf16[1,512,1152]{2,1,0:T(8,128)(2,1)S(1)} %dynamic-slice_bitcast_fusion.2), channel_id=1, source_target_pairs={{0,4},{4,0},{1,5},{5,1},{2,6},{6,2},{3,7},{7,3},{8,12},{12,8},{9,1... | collective-permute-start | bytes 3538952 | tf_op jit(solution)/shard_map/ppermute | solution.py:81
  156.0 11.4 %collective-permute-start.17 = (bf16[4,144,2304]{2,1,0:T(8,128)(2,1)}, bf16[4,144,2304]{2,1,0:T(8,128)(2,1)}, u32[]{:S(2)}, u32[]{:S(2)}) collective-permute-start(bf16[4,144,2304]{2,1,0:T(8,128)(2,1)} %bitcast_dynamic-update-slice_fusion.6), channel_id=1, source_target_pairs={{0,4},{4,0},{1,5},{5,1},{2,6},{6,2},{3,7},{7,3},{8,12},{12,8},{9,1... | collective-permute-start | bytes 7962632 | tf_op jit(solution)/shard_map/ppermute | solution.py:81
  156.3 83.1 %collective-permute-start.18 = (bf16[512,1152]{1,0:T(8,128)(2,1)}, bf16[512,1152]{1,0:T(8,128)(2,1)S(1)}, u32[]{:S(2)}, u32[]{:S(2)}) collective-permute-start(bf16[512,1152]{1,0:T(8,128)(2,1)} %bitcast.20), channel_id=1, source_target_pairs={{0,1},{1,2},{2,3},{3,0},{4,5},{5,6},{6,7},{7,4},{8,9},{9,10},{10,1... | collective-permute-start | bytes 3538952 | tf_op jit(solution)/shard_map/ppermute | solution.py:81
  159.0 104.7 %collective-permute-start.21 = (bf16[512,1152]{1,0:T(8,128)(2,1)}, bf16[512,1152]{1,0:T(8,128)(2,1)S(1)}, u32[]{:S(2)}, u32[]{:S(2)}) collective-permute-start(bf16[512,1152]{1,0:T(8,128)(2,1)} %bitcast.20), channel_id=1, source_target_pairs={{0,2},{1,3},{2,0},{3,1},{4,6},{5,7},{6,4},{7,5},{8,10},{9,11},{10,... | collective-permute-start | bytes 3538952 | tf_op jit(solution)/shard_map/ppermute | solution.py:81
  159.3 116.1 %collective-permute-start.24 = (bf16[512,1152]{1,0:T(8,128)(2,1)}, bf16[512,1152]{1,0:T(8,128)(2,1)S(1)}, u32[]{:S(2)}, u32[]{:S(2)}) collective-permute-start(bf16[512,1152]{1,0:T(8,128)(2,1)} %bitcast.20), channel_id=1, source_target_pairs={{0,3},{1,0},{2,1},{3,2},{4,7},{5,4},{6,5},{7,6},{8,11},{9,8},{10,9... | collective-permute-start | bytes 3538952 | tf_op jit(solution)/shard_map/ppermute | solution.py:81
  163.1 164.1 %copy-start.14 = (f32[512,1152]{1,0:T(8,128)}, f32[512,1152]{1,0:T(8,128)S(1)}, u32[]{:S(2)}) copy-start(f32[512,1152]{1,0:T(8,128)S(1)} %get-tuple-element.36) | copy-start | bytes 7077892
  164.0 72.1 %collective-permute-start.19 = (bf16[512,1152]{1,0:T(8,128)(2,1)S(1)}, bf16[512,1152]{1,0:T(8,128)(2,1)S(1)}, u32[]{:S(2)}, u32[]{:S(2)}) collective-permute-start(bf16[512,1152]{1,0:T(8,128)(2,1)S(1)} %multiply_convert_fusion), channel_id=1, source_target_pairs={{0,1},{1,2},{2,3},{3,0},{4,5},{5,6},{6,7},{7,4},{8,9},{9,10},{10,1... | collective-permute-start | bytes 3538952 | tf_op jit(solution)/shard_map/ppermute | solution.py:81
  167.4 94.0 %collective-permute-start.22 = (bf16[512,1152]{1,0:T(8,128)(2,1)S(1)}, bf16[512,1152]{1,0:T(8,128)(2,1)S(1)}, u32[]{:S(2)}, u32[]{:S(2)}) collective-permute-start(bf16[512,1152]{1,0:T(8,128)(2,1)S(1)} %multiply_convert_fusion), channel_id=1, source_target_pairs={{0,2},{1,3},{2,0},{3,1},{4,6},{5,7},{6,4},{7,5},{8,10},{9,11},{10,... | collective-permute-start | bytes 3538952 | tf_op jit(solution)/shard_map/ppermute | solution.py:81
  170.8 110.6 %copy-start.25 = (bf16[4,2,144,2304]{3,2,1,0:T(8,128)(2,1)}, bf16[4,2,144,2304]{3,2,1,0:T(8,128)(2,1)S(1)}, u32[]{:S(2)}) copy-start(bf16[4,2,144,2304]{3,2,1,0:T(8,128)(2,1)S(1)} %bitcast_dynamic-update-slice_fusion.1) | copy-start | bytes 15925252
  236.1 37.0 %collective-permute-start.25 = (bf16[512,1152]{1,0:T(8,128)(2,1)S(1)}, bf16[512,1152]{1,0:T(8,128)(2,1)S(1)}, u32[]{:S(2)}, u32[]{:S(2)}) collective-permute-start(bf16[512,1152]{1,0:T(8,128)(2,1)S(1)} %multiply_convert_fusion), channel_id=1, source_target_pairs={{0,3},{1,0},{2,1},{3,2},{4,7},{5,4},{6,5},{7,6},{8,11},{9,8},{10,9... | collective-permute-start | bytes 3538952 | tf_op jit(solution)/shard_map/ppermute | solution.py:81
  245.3 67.3 %collective-permute-start.20 = (bf16[512,1152]{1,0:T(8,128)(2,1)}, bf16[512,1152]{1,0:T(8,128)(2,1)}, u32[]{:S(2)}, u32[]{:S(2)}) collective-permute-start(bf16[512,1152]{1,0:T(8,128)(2,1)} %convolution_convert_fusion.9), channel_id=1, source_target_pairs={{0,3},{1,0},{2,1},{3,2},{4,7},{5,4},{6,5},{7,6},{8,11},{9,8},{10,9... | collective-permute-start | bytes 3538952 | tf_op jit(solution)/shard_map/ppermute | solution.py:81
  269.6 52.6 %collective-permute-start.23 = (bf16[512,1152]{1,0:T(8,128)(2,1)}, bf16[512,1152]{1,0:T(8,128)(2,1)}, u32[]{:S(2)}, u32[]{:S(2)}) collective-permute-start(bf16[512,1152]{1,0:T(8,128)(2,1)} %convolution_convert_fusion.8), channel_id=1, source_target_pairs={{0,2},{1,3},{2,0},{3,1},{4,6},{5,7},{6,4},{7,5},{8,10},{9,11},{10,... | collective-permute-start | bytes 3538952 | tf_op jit(solution)/shard_map/ppermute | solution.py:81
  281.2 41.1 %collective-permute-start.26 = (bf16[512,1152]{1,0:T(8,128)(2,1)}, bf16[512,1152]{1,0:T(8,128)(2,1)}, u32[]{:S(2)}, u32[]{:S(2)}) collective-permute-start(bf16[512,1152]{1,0:T(8,128)(2,1)} %convolution_convert_fusion.7), channel_id=1, source_target_pairs={{0,1},{1,2},{2,3},{3,0},{4,5},{5,6},{6,7},{7,4},{8,9},{9,10},{10,1... | collective-permute-start | bytes 3538952 | tf_op jit(solution)/shard_map/ppermute | solution.py:81
  300.7 30.6 %collective-permute-start.51 = (bf16[4,144,1536]{2,1,0:T(8,128)(2,1)S(1)}, bf16[4,144,1536]{2,1,0:T(8,128)(2,1)S(1)}, u32[]{:S(2)}, u32[]{:S(2)}) collective-permute-start(bf16[4,144,1536]{2,1,0:T(8,128)(2,1)S(1)} %dynamic-slice_bitcast_fusion), channel_id=1, source_target_pairs={{0,4},{4,0},{1,5},{5,1},{2,6},{6,2},{3,7},{7,3},{8,12},{12,8},{9,1... | collective-permute-start | bytes 5308424 | tf_op jit(solution)/shard_map/ppermute | solution.py:81
  305.4 173.0 %collective-permute-start.28 = (bf16[512,1152]{1,0:T(8,128)(2,1)}, bf16[512,1152]{1,0:T(8,128)(2,1)}, u32[]{:S(2)}, u32[]{:S(2)}) collective-permute-start(bf16[512,1152]{1,0:T(8,128)(2,1)} %convolution_convert_fusion.6), channel_id=1, source_target_pairs={{0,3},{1,0},{2,1},{3,2},{4,7},{5,4},{6,5},{7,6},{8,11},{9,8},{10,9... | collective-permute-start | bytes 3538952 | tf_op jit(solution)/shard_map/ppermute | solution.py:81
  329.4 44.9 %collective-permute-start.27 = (bf16[1,512,1152]{2,1,0:T(8,128)(2,1)S(1)}, bf16[1,512,1152]{2,1,0:T(8,128)(2,1)S(1)}, u32[]{:S(2)}, u32[]{:S(2)}) collective-permute-start(bf16[1,512,1152]{2,1,0:T(8,128)(2,1)S(1)} %get-tuple-element.33), channel_id=1, source_target_pairs={{0,4},{4,0},{1,5},{5,1},{2,6},{6,2},{3,7},{7,3},{8,12},{12,8},{9,1... | collective-permute-start | bytes 3538952 | tf_op jit(solution)/shard_map/ppermute | solution.py:81
  332.0 11.7 %collective-permute-start.52 = (bf16[144,1536]{1,0:T(8,128)(2,1)S(1)}, bf16[144,1536]{1,0:T(8,128)(2,1)S(1)}, u32[]{:S(2)}, u32[]{:S(2)}) collective-permute-start(bf16[144,1536]{1,0:T(8,128)(2,1)S(1)} %get-tuple-element.49), channel_id=1, source_target_pairs={{0,8},{8,16},{16,24},{24,0},{1,9},{9,17},{17,25},{25,1},{2,10},{10... | collective-permute-start | bytes 1327112 | tf_op jit(solution)/shard_map/ppermute | solution.py:81
  332.1 38.1 %collective-permute-start.53 = (bf16[144,1536]{1,0:T(8,128)(2,1)S(1)}, bf16[144,1536]{1,0:T(8,128)(2,1)S(1)}, u32[]{:S(2)}, u32[]{:S(2)}) collective-permute-start(bf16[144,1536]{1,0:T(8,128)(2,1)S(1)} %get-tuple-element.51), channel_id=1, source_target_pairs={{0,16},{8,24},{16,0},{24,8},{1,17},{9,25},{17,1},{25,9},{2,18},{10... | collective-permute-start | bytes 1327112 | tf_op jit(solution)/shard_map/ppermute | solution.py:81
  333.9 39.1 %collective-permute-start.54 = (bf16[144,1536]{1,0:T(8,128)(2,1)S(1)}, bf16[144,1536]{1,0:T(8,128)(2,1)S(1)}, u32[]{:S(2)}, u32[]{:S(2)}) collective-permute-start(bf16[144,1536]{1,0:T(8,128)(2,1)S(1)} %get-tuple-element.50), channel_id=1, source_target_pairs={{0,24},{8,0},{16,8},{24,16},{1,25},{9,1},{17,9},{25,17},{2,26},{10... | collective-permute-start | bytes 1327112 | tf_op jit(solution)/shard_map/ppermute | solution.py:81
  343.7 135.6 %collective-permute-start.29 = (bf16[512,1152]{1,0:T(8,128)(2,1)}, bf16[512,1152]{1,0:T(8,128)(2,1)}, u32[]{:S(2)}, u32[]{:S(2)}) collective-permute-start(bf16[512,1152]{1,0:T(8,128)(2,1)} %convolution_convert_fusion.5), channel_id=1, source_target_pairs={{0,2},{1,3},{2,0},{3,1},{4,6},{5,7},{6,4},{7,5},{8,10},{9,11},{10,... | collective-permute-start | bytes 3538952 | tf_op jit(solution)/shard_map/ppermute | solution.py:81
  370.2 109.1 %collective-permute-start.30 = (bf16[512,1152]{1,0:T(8,128)(2,1)}, bf16[512,1152]{1,0:T(8,128)(2,1)}, u32[]{:S(2)}, u32[]{:S(2)}) collective-permute-start(bf16[512,1152]{1,0:T(8,128)(2,1)} %convolution_convert_fusion.4), channel_id=1, source_target_pairs={{0,1},{1,2},{2,3},{3,0},{4,5},{5,6},{6,7},{7,4},{8,9},{9,10},{10,1... | collective-permute-start | bytes 3538952 | tf_op jit(solution)/shard_map/ppermute | solution.py:81
  388.5 32.3 %copy-start.20 = (f32[1024,64]{1,0:T(8,128)S(1)}, f32[1024,64]{1,0:T(8,128)}, u32[]{:S(2)}) copy-start(f32[1024,64]{1,0:T(8,128)} %copy-done.19) | copy-start | bytes 786436
  457.1 28.1 %collective-permute-start.44 = (f32[1152,2]{0,1:T(2,128)}, f32[1152,2]{0,1:T(2,128)}, u32[]{:S(2)}, u32[]{:S(2)}) collective-permute-start(f32[1152,2]{0,1:T(2,128)} %pad_maximum_fusion.5), channel_id=1, source_target_pairs={{0,4},{4,0},{1,5},{5,1},{2,6},{6,2},{3,7},{7,3},{8,12},{12,8},{9,1... | collective-permute-start | bytes 27656 | tf_op jit(solution)/shard_map/ppermute | solution.py:81
  460.9 37.8 %collective-permute-start.38 = (bf16[4,72,576]{2,1,0:T(8,128)(2,1)}, bf16[4,72,576]{2,1,0:T(8,128)(2,1)}, u32[]{:S(2)}, u32[]{:S(2)}) collective-permute-start(bf16[4,72,576]{2,1,0:T(8,128)(2,1)} %get-tuple-element.66), channel_id=1, source_target_pairs={{0,1},{1,2},{2,3},{3,0},{4,5},{5,6},{6,7},{7,4},{8,9},{9,10},{10,1... | collective-permute-start | bytes 995336 | tf_op jit(solution)/shard_map/ppermute | solution.py:81
  478.4 22.5 %collective-permute-start.39 = (bf16[4,72,576]{2,1,0:T(8,128)(2,1)}, bf16[4,72,576]{2,1,0:T(8,128)(2,1)}, u32[]{:S(2)}, u32[]{:S(2)}) collective-permute-start(bf16[4,72,576]{2,1,0:T(8,128)(2,1)} %get-tuple-element.68), channel_id=1, source_target_pairs={{0,2},{1,3},{2,0},{3,1},{4,6},{5,7},{6,4},{7,5},{8,10},{9,11},{10,... | collective-permute-start | bytes 995336 | tf_op jit(solution)/shard_map/ppermute | solution.py:81
  487.4 3.0 collective-permute-start.47
  489.6 2.4 collective-permute-start.46
  490.2 3.3 collective-permute-start.45
  493.5 2.8 collective-permute-start.48
  493.6 3.4 collective-permute-start.49
  494.9 2.9 collective-permute-start.50
  496.3 8.9 %collective-permute-start.40 = (bf16[4,72,576]{2,1,0:T(8,128)(2,1)}, bf16[4,72,576]{2,1,0:T(8,128)(2,1)S(1)}, u32[]{:S(2)}, u32[]{:S(2)}) collective-permute-start(bf16[4,72,576]{2,1,0:T(8,128)(2,1)} %get-tuple-element.67), channel_id=1, source_target_pairs={{0,3},{1,0},{2,1},{3,2},{4,7},{5,4},{6,5},{7,6},{8,11},{9,8},{10,9... | collective-permute-start | bytes 995336 | tf_op jit(solution)/shard_map/ppermute | solution.py:81
  497.0 19.8 %collective-permute-start.32 = (bf16[4,72,960]{2,1,0:T(8,128)(2,1)}, bf16[4,72,960]{2,1,0:T(8,128)(2,1)S(1)}, u32[]{:S(2)}, u32[]{:S(2)}) collective-permute-start(bf16[4,72,960]{2,1,0:T(8,128)(2,1)} %get-tuple-element.56), channel_id=1, source_target_pairs={{0,1},{1,2},{2,3},{3,0},{4,5},{5,6},{6,7},{7,4},{8,9},{9,10},{10,1... | collective-permute-start | bytes 1658888 | tf_op jit(solution)/shard_map/ppermute | solution.py:81
  497.8 22.7 %collective-permute-start.33 = (bf16[4,72,960]{2,1,0:T(8,128)(2,1)}, bf16[4,72,960]{2,1,0:T(8,128)(2,1)S(1)}, u32[]{:S(2)}, u32[]{:S(2)}) collective-permute-start(bf16[4,72,960]{2,1,0:T(8,128)(2,1)} %get-tuple-element.58), channel_id=1, source_target_pairs={{0,2},{1,3},{2,0},{3,1},{4,6},{5,7},{6,4},{7,5},{8,10},{9,11},{10,... | collective-permute-start | bytes 1658888 | tf_op jit(solution)/shard_map/ppermute | solution.py:81
  498.7 30.4 %collective-permute-start.34 = (bf16[4,72,960]{2,1,0:T(8,128)(2,1)}, bf16[4,72,960]{2,1,0:T(8,128)(2,1)S(1)}, u32[]{:S(2)}, u32[]{:S(2)}) collective-permute-start(bf16[4,72,960]{2,1,0:T(8,128)(2,1)} %get-tuple-element.57), channel_id=1, source_target_pairs={{0,3},{1,0},{2,1},{3,2},{4,7},{5,4},{6,5},{7,6},{8,11},{9,8},{10,9... | collective-permute-start | bytes 1658888 | tf_op jit(solution)/shard_map/ppermute | solution.py:81
  500.9 46.2 %collective-permute-start.55 = (bf16[4,144,768]{2,1,0:T(8,128)(2,1)}, bf16[4,144,768]{2,1,0:T(8,128)(2,1)S(1)}, u32[]{:S(2)}, u32[]{:S(2)}) collective-permute-start(bf16[4,144,768]{2,1,0:T(8,128)(2,1)} %dynamic-slice_bitcast_fusion.3), channel_id=1, source_target_pairs={{0,4},{4,0},{1,5},{5,1},{2,6},{6,2},{3,7},{7,3},{8,12},{12,8},{9,1... | collective-permute-start | bytes 2654216 | tf_op jit(solution)/shard_map/ppermute | solution.py:81
  505.2 64.5 %collective-permute-start.31 = (bf16[1,512,1152]{2,1,0:T(8,128)(2,1)S(1)}, bf16[1,512,1152]{2,1,0:T(8,128)(2,1)S(1)}, u32[]{:S(2)}, u32[]{:S(2)}) collective-permute-start(bf16[1,512,1152]{2,1,0:T(8,128)(2,1)S(1)} %dynamic-slice_bitcast_fusion.1), channel_id=1, source_target_pairs={{0,4},{4,0},{1,5},{5,1},{2,6},{6,2},{3,7},{7,3},{8,12},{12,8},{9,1... | collective-permute-start | bytes 3538952 | tf_op jit(solution)/shard_map/ppermute | solution.py:81
  516.8 14.0 %collective-permute-start.41 = (bf16[72,576]{1,0:T(8,128)(2,1)S(1)}, bf16[72,576]{1,0:T(8,128)(2,1)S(1)}, u32[]{:S(2)}, u32[]{:S(2)}) collective-permute-start(bf16[72,576]{1,0:T(8,128)(2,1)S(1)} %get-tuple-element.74), channel_id=1, source_target_pairs={{0,8},{8,16},{16,24},{24,0},{1,9},{9,17},{17,25},{25,1},{2,10},{10... | collective-permute-start | bytes 248840 | tf_op jit(solution)/shard_map/ppermute | solution.py:81
  520.4 10.6 %collective-permute-start.42 = (bf16[72,576]{1,0:T(8,128)(2,1)S(1)}, bf16[72,576]{1,0:T(8,128)(2,1)S(1)}, u32[]{:S(2)}, u32[]{:S(2)}) collective-permute-start(bf16[72,576]{1,0:T(8,128)(2,1)S(1)} %get-tuple-element.76), channel_id=1, source_target_pairs={{0,16},{8,24},{16,0},{24,8},{1,17},{9,25},{17,1},{25,9},{2,18},{10... | collective-permute-start | bytes 248840 | tf_op jit(solution)/shard_map/ppermute | solution.py:81
  529.1 5.0 collective-permute-start.43
  530.8 4.2 collective-permute-start.35
  531.1 13.5 %collective-permute-start.36 = (bf16[72,960]{1,0:T(8,128)(2,1)S(1)}, bf16[72,960]{1,0:T(8,128)(2,1)S(1)}, u32[]{:S(2)}, u32[]{:S(2)}) collective-permute-start(bf16[72,960]{1,0:T(8,128)(2,1)S(1)} %get-tuple-element.71), channel_id=1, source_target_pairs={{0,16},{8,24},{16,0},{24,8},{1,17},{9,25},{17,1},{25,9},{2,18},{10... | collective-permute-start | bytes 414728 | tf_op jit(solution)/shard_map/ppermute | solution.py:81
  534.1 12.2 %collective-permute-start.37 = (bf16[72,960]{1,0:T(8,128)(2,1)S(1)}, bf16[72,960]{1,0:T(8,128)(2,1)S(1)}, u32[]{:S(2)}, u32[]{:S(2)}) collective-permute-start(bf16[72,960]{1,0:T(8,128)(2,1)S(1)} %get-tuple-element.70), channel_id=1, source_target_pairs={{0,24},{8,0},{16,8},{24,16},{1,25},{9,1},{17,9},{25,17},{2,26},{10... | collective-permute-start | bytes 414728 | tf_op jit(solution)/shard_map/ppermute | solution.py:81
  547.4 4.8 collective-permute-start.56
  547.5 16.8 %collective-permute-start.57 = (bf16[144,768]{1,0:T(8,128)(2,1)S(1)}, bf16[144,768]{1,0:T(8,128)(2,1)S(1)}, u32[]{:S(2)}, u32[]{:S(2)}) collective-permute-start(bf16[144,768]{1,0:T(8,128)(2,1)S(1)} %get-tuple-element.61), channel_id=1, source_target_pairs={{0,16},{8,24},{16,0},{24,8},{1,17},{9,25},{17,1},{25,9},{2,18},{10... | collective-permute-start | bytes 663560 | tf_op jit(solution)/shard_map/ppermute | solution.py:81
  548.7 20.1 %collective-permute-start.58 = (bf16[144,768]{1,0:T(8,128)(2,1)S(1)}, bf16[144,768]{1,0:T(8,128)(2,1)S(1)}, u32[]{:S(2)}, u32[]{:S(2)}) collective-permute-start(bf16[144,768]{1,0:T(8,128)(2,1)S(1)} %get-tuple-element.60), channel_id=1, source_target_pairs={{0,24},{8,0},{16,8},{24,16},{1,25},{9,1},{17,9},{25,17},{2,26},{10... | collective-permute-start | bytes 663560 | tf_op jit(solution)/shard_map/ppermute | solution.py:81
  (74 other events, 440.6 us)

commit v2 on v1

--- a/solution.py
+++ b/solution.py
@@ -256,8 +256,13 @@
     own_qkv = jnp.concatenate(
         [w_query, w_key, w_value, norm_first[:, None], norm_second[:, None]], axis=1
     )
-    qkv_all = gather_two(own_qkv, "fsdp", "tensor")
+    ffn_own = jnp.concatenate([w_gate, w_up, w_down.T], axis=1)
+    qkv_major = gather_at(own_qkv, "fsdp", 0)
+    qkv_major, ffn_own = lax.optimization_barrier((qkv_major, ffn_own))
+    qkv_all = gather_at(qkv_major, "tensor", 1).reshape(model_width, -1)
     out_t = gather_two(w_out.T, "fsdp", "tensor")
+    down_grad = cotangent.reshape(blocks * half_len, model_width)
+    qkv_all, down_grad = lax.optimization_barrier((qkv_all, down_grad))
     qkv_w = qkv_all[:, :qkv_width]
     gain_one = qkv_all[:, qkv_width].astype(jnp.float32)
     gain_two = qkv_all[:, qkv_width + 1].astype(jnp.float32)
@@ -267,9 +272,6 @@
     normed_one = (rows_one * scale_one * gain_one).astype(jnp.bfloat16)
     projected = jnp.dot(normed_one, qkv_w, preferred_element_type=jnp.float32)
 
-    down_grad = cotangent.reshape(blocks * half_len, model_width)
-    ffn_own = jnp.concatenate([w_gate, w_up, w_down.T], axis=1)
-    projected, down_grad, ffn_own = lax.optimization_barrier((projected, down_grad, ffn_own))
     ffn_w = gather_two(ffn_own, "fsdp", "heads")
     gate_up_w = ffn_w[:, : 2 * inner]
     down_t = ffn_w[:, 2 * inner :]

time: 580 us -> 592 us (1.021)
  waiting for transfers between devices: 207 us -> 230 us
  local copies, waits for them, and re-layouts: 83.9 us -> 76 us
    ppermute x59, waiting for transfers between devices: 207 us -> 230 us  [shifted(): lax.ppermute(value, axis, [(i, (i + step) % size) for i in range(size)])]
    dynamic_update_slice x25, local copies, waits for them, and re-layouts: 26.6 us -> 17.6 us  [gather_at(): lax.dynamic_update_slice_in_dim(whole, jnp.expand_dims(part, place), (me...]
    unnamed x165 -> x173, local copies, waits for them, and re-layouts: 12.5 us -> 15.2 us
  transfers between devices with their start and end apart: 59 -> 59, of which waited for: 24 -> 25; matrix products, arithmetic and copies ran while one was open for 37% -> 35% of each run, Pallas kernels for 9% -> 9%
where the time goes in v2:
time: 592 us; the launch traced here: 583 us
  waiting for transfers between devices  230 us (39%)
  matrix products  92.8 us (16%)
  local copies, waits for them, and re-layouts  76 us (13%)
  starting transfers between devices  73.4 us (12%)
  other arithmetic  54.9 us (9%)
  Pallas kernels  53.1 us (9%)
    ppermute x59, waiting for transfers between devices, shifted(): lax.ppermute(value, axis, [(i, (i + step) % size) for i in range(size)])  230 us
    ppermute x59, starting transfers between devices, shifted(): lax.ppermute(value, axis, [(i, (i + step) % size) for i in range(size)])  73.4 us
    dot_general x10, matrix products, dot_last(): lax.dot_general(left_side, right_side, (((1,), (1,)), ((), ())), preferre...  40.8 us
    pallas_call x1, Pallas kernels, attention_back(): pl.pallas_call(attention_back_kernel, grid=(heads,), in_specs=[at_start,...  32.3 us
    dot_general x4, matrix products, contract_rows(): lax.dot_general(left_side, right_side, (((0,), (0,)), ((), ())), preferre...  26.4 us
    pallas_call x1, Pallas kernels, attention(): pl.pallas_call(attention_kernel, grid=(heads,), in_specs=[at_start, at_qu...  20.8 us
    dynamic_update_slice x25, local copies, waits for them, and re-layouts, gather_at(): lax.dynamic_update_slice_in_dim(whole, jnp.expand_dims(part, place), (me...  17.6 us
    unnamed x173, local copies, waits for them, and re-layouts  15.2 us
  transfers between devices with their start and end apart: 59, of which 25 were waited for; matrix products, arithmetic and copies ran while one was open for 35% of the time, Pallas kernels for 9%

profile of v2, /device:TPU:9, one launch (start us, length us, event | category | flops | bytes accessed | tf_op | source)
XLA Modules:
  0.0 583.0 jit_solution(16073846284805704205)
XLA Ops:
  16.2 2.5 collective-permute-done.7
  40.0 7.7 %collective-permute-done.11 = bf16[4,72,576]{2,1,0:T(8,128)(2,1)S(1)} collective-permute-done((bf16[4,72,576]{2,1,0:T(8,128)(2,1)}, bf16[4,72,576]{2,1,0:T(8,128)(2,1)S(1)}, u32[]{:S(2)}, u32[]{:S(2)}) %collective-permute-start.11) | collective-permute-done | bytes 331808 | tf_op jit(solution)/shard_map/ppermute | solution.py:81
  49.8 6.2 %collective-permute-done.4 = bf16[4,72,962]{2,1,0:T(8,128)(2,1)S(1)} collective-permute-done((bf16[4,72,962]{2,1,0:T(8,128)(2,1)S(1)}, bf16[4,72,962]{2,1,0:T(8,128)(2,1)S(1)}, u32[]{:S(2)}, u32[]{:S(2)}) %collective-permute-start.4) | collective-permute-done | bytes 554144 | tf_op jit(solution)/shard_map/ppermute | solution.py:81
  56.0 2.4 collective-permute-start.15
  58.4 12.6 %collective-permute-done.5 = bf16[4,72,962]{2,1,0:T(8,128)(2,1)S(1)} collective-permute-done((bf16[4,72,962]{2,1,0:T(8,128)(2,1)S(1)}, bf16[4,72,962]{2,1,0:T(8,128)(2,1)S(1)}, u32[]{:S(2)}, u32[]{:S(2)}) %collective-permute-start.5) | collective-permute-done | bytes 554144 | tf_op jit(solution)/shard_map/ppermute | solution.py:81
  71.0 2.5 collective-permute-start.16
  75.4 24.2 %collective-permute-done.15 = bf16[144,2304]{1,0:T(8,128)(2,1)S(1)} collective-permute-done((bf16[144,2304]{1,0:T(8,128)(2,1)S(1)}, bf16[144,2304]{1,0:T(8,128)(2,1)S(1)}, u32[]{:S(2)}, u32[]{:S(2)}) %collective-permute-start.15) | collective-permute-done | bytes 663584 | tf_op jit(solution)/shard_map/ppermute | solution.py:81
  106.9 2.8 fusion.66
  114.8 5.2 copy.154
  120.0 8.8 %slice_negate_fusion.1 = (f32[1,1024,9,32]{3,1,2,0:T(8,128)}, f32[1,1024,9,32]{3,1,2,0:T(8,128)}) fusion(f32[1,1024,9,64]{3,1,2,0:T(8,128)} %copy.154), kind=kLoop, calls=%fused_computation.17 | loop fusion | flops 294912 | bytes 4718592 | tf_op jit(solution)/shard_map/neg | solution.py:61
  130.2 2.7 fusion.92.key_ref
  133.7 5.2 fusion.60.query_ref
  139.0 20.8 %attention.1 = bf16[9,1024,64]{2,1,0:T(8,128)(2,1)S(1)} custom-call(s32[1024,1]{1,0:T(8,128)S(1)} %copy-done.7, bf16[9,1024,64]{2,1,0:T(8,128)(2,1)S(1)} %fusion.60.query_ref, bf16[3,1024,64]{2,1,0:T(8,128)(2,1)S(1)} %fusion.92.key_ref, bf16[3,1024,64]{2,1,0:T(8,128)(2,1)S(1)} %bitcast.325), custom_call_target="tpu_custom_call" | custom-call | flops 2264924160 | bytes 4718592 | tf_op jit(solution)/shard_map/attention/pallas_call | solution.py:194
  161.9 3.9 convolution_convert_fusion.1
  178.8 2.2 fusion.105
  181.1 4.4 multiply_convert_fusion.11
  185.5 61.0 %collective-permute-done.19 = bf16[512,1152]{1,0:T(8,128)(2,1)S(1)} collective-permute-done((bf16[512,1152]{1,0:T(8,128)(2,1)S(1)}, bf16[512,1152]{1,0:T(8,128)(2,1)S(1)}, u32[]{:S(2)}, u32[]{:S(2)}) %collective-permute-start.19) | collective-permute-done | bytes 1179680 | tf_op jit(solution)/shard_map/ppermute | solution.py:81
  246.6 2.2 fusion.102
  248.8 2.6 multiply_convert_fusion.9
  251.4 3.3 convolution_convert_fusion.9
  254.7 2.3 collective-permute-start.20
  257.0 15.4 %collective-permute-done.22 = bf16[512,1152]{1,0:T(8,128)(2,1)S(1)} collective-permute-done((bf16[512,1152]{1,0:T(8,128)(2,1)S(1)}, bf16[512,1152]{1,0:T(8,128)(2,1)S(1)}, u32[]{:S(2)}, u32[]{:S(2)}) %collective-permute-start.22) | collective-permute-done | bytes 1179680 | tf_op jit(solution)/shard_map/ppermute | solution.py:81
  272.4 2.2 fusion.99
  274.6 2.6 multiply_convert_fusion.7
  277.3 3.3 convolution_convert_fusion.8
  282.8 2.6 multiply_convert_fusion.5
  285.4 3.3 convolution_convert_fusion.7
  288.8 13.1 %convolution_convert_fusion = bf16[1152,1536]{1,0:T(8,128)(2,1)} fusion(bf16[512,768]{1,0:T(8,128)(2,1)} %copy-done.80, bf16[512,768]{1,0:T(8,128)(2,1)} %copy-done.79, bf16[512,768]{1,0:T(8,128)(2,1)} %copy-done.78, bf16[512,768]{1,0:T(8,128)(2,1)} %copy-done.77, bf16[512,768]{1,0:T(8,128)(2,1)} %copy-done.76, bf16[512,768]{1,0:T(8,128)(2,1)} %copy-done.75, ...), kind=kOutput, calls=%fused_computation | convolution fusion | flops 7318732800 | bytes 14548992 | tf_op jit(solution)/shard_map/dot_general | solution.py:19
  304.9 3.9 convolution_convert_fusion.6
  308.8 2.9 collective-permute-start.28
  311.7 2.2 convolution_convert_fusion.5
  313.9 2.3 convolution_convert_fusion.4
  316.2 16.9 %collective-permute-done.23 = bf16[512,1152]{1,0:T(8,128)(2,1)} collective-permute-done((bf16[512,1152]{1,0:T(8,128)(2,1)}, bf16[512,1152]{1,0:T(8,128)(2,1)}, u32[]{:S(2)}, u32[]{:S(2)}) %collective-permute-start.23) | collective-permute-done | bytes 1179680 | tf_op jit(solution)/shard_map/ppermute | solution.py:81
  333.2 4.8 multiply_reduce_fusion
  343.0 3.2 collective-permute-start.53
  348.0 6.6 %collective-permute-done.52 = bf16[144,1536]{1,0:T(8,128)(2,1)S(1)} collective-permute-done((bf16[144,1536]{1,0:T(8,128)(2,1)S(1)}, bf16[144,1536]{1,0:T(8,128)(2,1)S(1)}, u32[]{:S(2)}, u32[]{:S(2)}) %collective-permute-start.52) | collective-permute-done | bytes 442400 | tf_op jit(solution)/shard_map/ppermute | solution.py:81
  354.6 26.5 %collective-permute-done.53 = bf16[144,1536]{1,0:T(8,128)(2,1)S(1)} collective-permute-done((bf16[144,1536]{1,0:T(8,128)(2,1)S(1)}, bf16[144,1536]{1,0:T(8,128)(2,1)S(1)}, u32[]{:S(2)}, u32[]{:S(2)}) %collective-permute-start.53) | collective-permute-done | bytes 442400 | tf_op jit(solution)/shard_map/ppermute | solution.py:81
  381.6 3.7 collective-permute-done.54
  389.0 2.8 convolution_convert_fusion.3
  391.7 2.4 copy.167
  400.8 32.3 %attention_back.1 = (f32[9,1024,64]{2,1,0:T(8,128)}, f32[3,1024,64]{2,1,0:T(8,128)S(1)}, f32[3,1024,64]{2,1,0:T(8,128)S(1)}) custom-call(s32[1024,1]{1,0:T(8,128)S(1)} %copy-done.8, bf16[9,1024,64]{2,1,0:T(8,128)(2,1)S(1)} %copy-done.1, bf16[3,1024,64]{2,1,0:T(8,128)(2,1)S(1)} %copy-done.4, bf16[3,1024,64]{2,1,0:T(8,128)(2,1)S(1)} %bitcast.326, ...), custom_call_target="tpu_custom_call" | custom-call | flops 9059696640 | bytes 9437184 | tf_op jit(solution)/shard_map/attention_back/pallas_call | solution.py:212
  433.1 2.9 fusion.33
  436.0 3.7 fusion.155
  439.7 5.1 fusion.17
  444.8 4.0 copy.169
  452.3 2.2 copy.170
  455.0 8.3 %fusion.42 = (f32[1152]{0:T(1024)S(1)}, f32[1024]{0:T(1024)S(1)}, f32[1024,1152]{1,0:T(8,128)}) fusion(bf16[1,2,512,1152]{3,2,1,0:T(8,128)(2,1)} %copy-done.10, f32[1024]{0:T(1024)S(1)} %bitcast.382, f32[1152]{0:T(1024)S(1)} %copy-done.50, bf16[1152,962]{1,0:T(8,128)(2,1)} %bitcast.354, bf16[1024,192]{0,1:T(8,128)(2,1)S(1)} %bitcast.374, ...), kind=kOutput, calls=%fused_computation.54 | convolution fusion | flops 2279077888 | bytes 11277824 | tf_op jit(solution)/shard_map/dot_general | solution.py:74
  463.4 5.1 convolution_convert_fusion.2
  472.8 4.6 copy.172
  477.5 3.2 fusion.39
  484.5 5.4 fusion.43
  490.1 5.4 fusion.59
  498.7 2.2 collective-permute-start.47
  512.2 4.0 collective-permute-start.55
  516.2 6.7 %collective-permute-start.31 = (bf16[1,512,1152]{2,1,0:T(8,128)(2,1)S(1)}, bf16[1,512,1152]{2,1,0:T(8,128)(2,1)S(1)}, u32[]{:S(2)}, u32[]{:S(2)}) collective-permute-start(bf16[1,512,1152]{2,1,0:T(8,128)(2,1)S(1)} %dynamic-slice_bitcast_fusion.1), channel_id=1, source_target_pairs={{0,4},{4,0},{1,5},{5,1},{2,6},{6,2},{3,7},{7,3},{8,12},{12,8},{9,1... | collective-permute-start | bytes 3538952 | tf_op jit(solution)/shard_map/ppermute | solution.py:81
  524.3 3.4 collective-permute-done.32
  528.7 3.1 collective-permute-done.33
  531.9 5.1 collective-permute-start.42
  536.9 2.8 collective-permute-done.34
  542.2 3.2 collective-permute-start.36
  546.6 7.8 %collective-permute-done.36 = bf16[72,960]{1,0:T(8,128)(2,1)S(1)} collective-permute-done((bf16[72,960]{1,0:T(8,128)(2,1)S(1)}, bf16[72,960]{1,0:T(8,128)(2,1)S(1)}, u32[]{:S(2)}, u32[]{:S(2)}) %collective-permute-start.36) | collective-permute-done | bytes 138272 | tf_op jit(solution)/shard_map/ppermute | solution.py:81
  554.4 3.3 collective-permute-done.37
  563.6 12.0 %collective-permute-done.57 = bf16[144,768]{1,0:T(8,128)(2,1)S(1)} collective-permute-done((bf16[144,768]{1,0:T(8,128)(2,1)S(1)}, bf16[144,768]{1,0:T(8,128)(2,1)S(1)}, u32[]{:S(2)}, u32[]{:S(2)}) %collective-permute-start.57) | collective-permute-done | bytes 221216 | tf_op jit(solution)/shard_map/ppermute | solution.py:81
  575.6 4.6 collective-permute-done.58
  (369 shorter events, 134.2 us)
Async XLA Ops:
  3.3 26.6 %collective-permute-start.1 = (bf16[72,962]{1,0:T(8,128)(2,1)S(1)}, bf16[72,962]{1,0:T(8,128)(2,1)}, u32[]{:S(2)}, u32[]{:S(2)}) collective-permute-start(bf16[72,962]{1,0:T(8,128)(2,1)S(1)} %concatenate.64), channel_id=1, source_target_pairs={{0,8},{8,16},{16,24},{24,0},{1,9},{9,17},{17,25},{25,1},{2,10},{10... | collective-permute-start | bytes 415592 | tf_op jit(solution)/shard_map/ppermute | solution.py:81
  4.6 27.5 %collective-permute-start.2 = (bf16[72,962]{1,0:T(8,128)(2,1)S(1)}, bf16[72,962]{1,0:T(8,128)(2,1)}, u32[]{:S(2)}, u32[]{:S(2)}) collective-permute-start(bf16[72,962]{1,0:T(8,128)(2,1)S(1)} %concatenate.64), channel_id=1, source_target_pairs={{0,16},{8,24},{16,0},{24,8},{1,17},{9,25},{17,1},{25,9},{2,18},{10... | collective-permute-start | bytes 415592 | tf_op jit(solution)/shard_map/ppermute | solution.py:81
  5.7 28.5 %collective-permute-start.3 = (bf16[72,962]{1,0:T(8,128)(2,1)S(1)}, bf16[72,962]{1,0:T(8,128)(2,1)}, u32[]{:S(2)}, u32[]{:S(2)}) collective-permute-start(bf16[72,962]{1,0:T(8,128)(2,1)S(1)} %concatenate.64), channel_id=1, source_target_pairs={{0,24},{8,0},{16,8},{24,16},{1,25},{9,1},{17,9},{25,17},{2,26},{10... | collective-permute-start | bytes 415592 | tf_op jit(solution)/shard_map/ppermute | solution.py:81
  7.1 96.2 %collective-permute-start = (bf16[1,512,1152]{2,1,0:T(8,128)(2,1)}, bf16[1,512,1152]{2,1,0:T(8,128)(2,1)}, u32[]{:S(2)}, u32[]{:S(2)}) collective-permute-start(bf16[1,512,1152]{2,1,0:T(8,128)(2,1)} %param.12), channel_id=1, source_target_pairs={{0,4},{4,0},{1,5},{5,1},{2,6},{6,2},{3,7},{7,3},{8,12},{12,8},{9,1... | collective-permute-start | bytes 3538952 | tf_op jit(solution)/shard_map/ppermute | solution.py:81
  8.6 10.1 %collective-permute-start.7 = (bf16[72,576]{1,0:T(8,128)(2,1)}, bf16[72,576]{1,0:T(8,128)(2,1)}, u32[]{:S(2)}, u32[]{:S(2)}) collective-permute-start(bf16[72,576]{1,0:T(8,128)(2,1)} %bitcast.377), channel_id=1, source_target_pairs={{0,8},{8,16},{16,24},{24,0},{1,9},{9,17},{17,25},{25,1},{2,10},{10... | collective-permute-start | bytes 248840 | tf_op jit(solution)/shard_map/ppermute | solution.py:81
  16.2 116.7 %copy-start.16 = (f32[1024,64]{1,0:T(8,128)}, f32[1024,64]{1,0:T(8,128)S(1)}, u32[]{:S(2)}) copy-start(f32[1024,64]{1,0:T(8,128)S(1)} %get-tuple-element.79) | copy-start | bytes 786436
  16.2 116.7 %copy-start.19 = (f32[1024,64]{1,0:T(8,128)}, f32[1024,64]{1,0:T(8,128)S(1)}, u32[]{:S(2)}) copy-start(f32[1024,64]{1,0:T(8,128)S(1)} %get-tuple-element.80) | copy-start | bytes 786436
  18.7 4.4 collective-permute-start.8
  23.1 3.7 collective-permute-start.9
  27.5 12.1 %collective-permute-start.10 = (bf16[4,72,576]{2,1,0:T(8,128)(2,1)}, bf16[4,72,576]{2,1,0:T(8,128)(2,1)S(1)}, u32[]{:S(2)}, u32[]{:S(2)}) collective-permute-start(bf16[4,72,576]{2,1,0:T(8,128)(2,1)} %bitcast_dynamic-update-slice_fusion.23), channel_id=1, source_target_pairs={{0,1},{1,2},{2,3},{3,0},{4,5},{5,6},{6,7},{7,4},{8,9},{9,10},{10,1... | collective-permute-start | bytes 995336 | tf_op jit(solution)/shard_map/ppermute | solution.py:81
  29.9 17.8 %collective-permute-start.11 = (bf16[4,72,576]{2,1,0:T(8,128)(2,1)}, bf16[4,72,576]{2,1,0:T(8,128)(2,1)S(1)}, u32[]{:S(2)}, u32[]{:S(2)}) collective-permute-start(bf16[4,72,576]{2,1,0:T(8,128)(2,1)} %bitcast_dynamic-update-slice_fusion.23), channel_id=1, source_target_pairs={{0,2},{1,3},{2,0},{3,1},{4,6},{5,7},{6,4},{7,5},{8,10},{9,11},{10,... | collective-permute-start | bytes 995336 | tf_op jit(solution)/shard_map/ppermute | solution.py:81
  32.1 17.6 %collective-permute-start.12 = (bf16[4,72,576]{2,1,0:T(8,128)(2,1)}, bf16[4,72,576]{2,1,0:T(8,128)(2,1)S(1)}, u32[]{:S(2)}, u32[]{:S(2)}) collective-permute-start(bf16[4,72,576]{2,1,0:T(8,128)(2,1)} %bitcast_dynamic-update-slice_fusion.23), channel_id=1, source_target_pairs={{0,3},{1,0},{2,1},{3,2},{4,7},{5,4},{6,5},{7,6},{8,11},{9,8},{10,9... | collective-permute-start | bytes 995336 | tf_op jit(solution)/shard_map/ppermute | solution.py:81
  35.2 39.0 %collective-permute-start.14 = (bf16[144,2304]{1,0:T(8,128)(2,1)S(1)}, bf16[144,2304]{1,0:T(8,128)(2,1)S(1)}, u32[]{:S(2)}, u32[]{:S(2)}) collective-permute-start(bf16[144,2304]{1,0:T(8,128)(2,1)S(1)} %pad_maximum_fusion.3), channel_id=1, source_target_pairs={{0,8},{8,16},{16,24},{24,0},{1,9},{9,17},{17,25},{25,1},{2,10},{10... | collective-permute-start | bytes 1990664 | tf_op jit(solution)/shard_map/ppermute | solution.py:81
  39.6 16.4 %collective-permute-start.4 = (bf16[4,72,962]{2,1,0:T(8,128)(2,1)S(1)}, bf16[4,72,962]{2,1,0:T(8,128)(2,1)S(1)}, u32[]{:S(2)}, u32[]{:S(2)}) collective-permute-start(bf16[4,72,962]{2,1,0:T(8,128)(2,1)S(1)} %bitcast_dynamic-update-slice_fusion.18), channel_id=1, source_target_pairs={{0,1},{1,2},{2,3},{3,0},{4,5},{5,6},{6,7},{7,4},{8,9},{9,10},{10,1... | collective-permute-start | bytes 1662344 | tf_op jit(solution)/shard_map/ppermute | solution.py:81
  47.7 23.3 %collective-permute-start.5 = (bf16[4,72,962]{2,1,0:T(8,128)(2,1)S(1)}, bf16[4,72,962]{2,1,0:T(8,128)(2,1)S(1)}, u32[]{:S(2)}, u32[]{:S(2)}) collective-permute-start(bf16[4,72,962]{2,1,0:T(8,128)(2,1)S(1)} %bitcast_dynamic-update-slice_fusion.18), channel_id=1, source_target_pairs={{0,2},{1,3},{2,0},{3,1},{4,6},{5,7},{6,4},{7,5},{8,10},{9,11},{10,... | collective-permute-start | bytes 1662344 | tf_op jit(solution)/shard_map/ppermute | solution.py:81
  49.7 23.9 %collective-permute-start.6 = (bf16[4,72,962]{2,1,0:T(8,128)(2,1)S(1)}, bf16[4,72,962]{2,1,0:T(8,128)(2,1)S(1)}, u32[]{:S(2)}, u32[]{:S(2)}) collective-permute-start(bf16[4,72,962]{2,1,0:T(8,128)(2,1)S(1)} %bitcast_dynamic-update-slice_fusion.18), channel_id=1, source_target_pairs={{0,3},{1,0},{2,1},{3,2},{4,7},{5,4},{6,5},{7,6},{8,11},{9,8},{10,9... | collective-permute-start | bytes 1662344 | tf_op jit(solution)/shard_map/ppermute | solution.py:81
  56.0 43.5 %collective-permute-start.15 = (bf16[144,2304]{1,0:T(8,128)(2,1)S(1)}, bf16[144,2304]{1,0:T(8,128)(2,1)S(1)}, u32[]{:S(2)}, u32[]{:S(2)}) collective-permute-start(bf16[144,2304]{1,0:T(8,128)(2,1)S(1)} %pad_maximum_fusion.3), channel_id=1, source_target_pairs={{0,16},{8,24},{16,0},{24,8},{1,17},{9,25},{17,1},{25,9},{2,18},{10... | collective-permute-start | bytes 1990664 | tf_op jit(solution)/shard_map/ppermute | solution.py:81
  71.0 29.4 %collective-permute-start.16 = (bf16[144,2304]{1,0:T(8,128)(2,1)S(1)}, bf16[144,2304]{1,0:T(8,128)(2,1)S(1)}, u32[]{:S(2)}, u32[]{:S(2)}) collective-permute-start(bf16[144,2304]{1,0:T(8,128)(2,1)S(1)} %pad_maximum_fusion.3), channel_id=1, source_target_pairs={{0,24},{8,0},{16,8},{24,16},{1,25},{9,1},{17,9},{25,17},{2,26},{10... | collective-permute-start | bytes 1990664 | tf_op jit(solution)/shard_map/ppermute | solution.py:81
  73.7 33.2 %copy-start.29 = (bf16[4,4,72,962]{3,2,1,0:T(8,128)(2,1)}, bf16[4,4,72,962]{3,2,1,0:T(8,128)(2,1)S(1)}, u32[]{:S(2)}) copy-start(bf16[4,4,72,962]{3,2,1,0:T(8,128)(2,1)S(1)} %bitcast_dynamic-update-slice_fusion.13) | copy-start | bytes 6649348
  101.3 74.9 %collective-permute-start.17 = (bf16[4,144,2304]{2,1,0:T(8,128)(2,1)}, bf16[4,144,2304]{2,1,0:T(8,128)(2,1)}, u32[]{:S(2)}, u32[]{:S(2)}) collective-permute-start(bf16[4,144,2304]{2,1,0:T(8,128)(2,1)} %bitcast_dynamic-update-slice_fusion.6), channel_id=1, source_target_pairs={{0,4},{4,0},{1,5},{5,1},{2,6},{6,2},{3,7},{7,3},{8,12},{12,8},{9,1... | collective-permute-start | bytes 7962632 | tf_op jit(solution)/shard_map/ppermute | solution.py:81
  167.4 6.8 %collective-permute-start.13 = (bf16[1,512,1152]{2,1,0:T(8,128)(2,1)S(1)}, bf16[1,512,1152]{2,1,0:T(8,128)(2,1)S(1)}, u32[]{:S(2)}, u32[]{:S(2)}) collective-permute-start(bf16[1,512,1152]{2,1,0:T(8,128)(2,1)S(1)} %dynamic-slice_bitcast_fusion.2), channel_id=1, source_target_pairs={{0,4},{4,0},{1,5},{5,1},{2,6},{6,2},{3,7},{7,3},{8,12},{12,8},{9,1... | collective-permute-start | bytes 3538952 | tf_op jit(solution)/shard_map/ppermute | solution.py:81
  167.5 81.3 %collective-permute-start.18 = (bf16[512,1152]{1,0:T(8,128)(2,1)}, bf16[512,1152]{1,0:T(8,128)(2,1)S(1)}, u32[]{:S(2)}, u32[]{:S(2)}) collective-permute-start(bf16[512,1152]{1,0:T(8,128)(2,1)} %bitcast.21), channel_id=1, source_target_pairs={{0,1},{1,2},{2,3},{3,0},{4,5},{5,6},{6,7},{7,4},{8,9},{9,10},{10,1... | collective-permute-start | bytes 3538952 | tf_op jit(solution)/shard_map/ppermute | solution.py:81
  168.7 106.0 %collective-permute-start.21 = (bf16[512,1152]{1,0:T(8,128)(2,1)}, bf16[512,1152]{1,0:T(8,128)(2,1)S(1)}, u32[]{:S(2)}, u32[]{:S(2)}) collective-permute-start(bf16[512,1152]{1,0:T(8,128)(2,1)} %bitcast.21), channel_id=1, source_target_pairs={{0,2},{1,3},{2,0},{3,1},{4,6},{5,7},{6,4},{7,5},{8,10},{9,11},{10,... | collective-permute-start | bytes 3538952 | tf_op jit(solution)/shard_map/ppermute | solution.py:81
  168.9 113.9 %collective-permute-start.24 = (bf16[512,1152]{1,0:T(8,128)(2,1)}, bf16[512,1152]{1,0:T(8,128)(2,1)S(1)}, u32[]{:S(2)}, u32[]{:S(2)}) collective-permute-start(bf16[512,1152]{1,0:T(8,128)(2,1)} %bitcast.21), channel_id=1, source_target_pairs={{0,3},{1,0},{2,1},{3,2},{4,7},{5,4},{6,5},{7,6},{8,11},{9,8},{10,9... | collective-permute-start | bytes 3538952 | tf_op jit(solution)/shard_map/ppermute | solution.py:81
  174.8 163.3 %copy-start.14 = (f32[512,1152]{1,0:T(8,128)}, f32[512,1152]{1,0:T(8,128)S(1)}, u32[]{:S(2)}) copy-start(f32[512,1152]{1,0:T(8,128)S(1)} %get-tuple-element.38) | copy-start | bytes 7077892
  175.7 70.8 %collective-permute-start.19 = (bf16[512,1152]{1,0:T(8,128)(2,1)S(1)}, bf16[512,1152]{1,0:T(8,128)(2,1)S(1)}, u32[]{:S(2)}, u32[]{:S(2)}) collective-permute-start(bf16[512,1152]{1,0:T(8,128)(2,1)S(1)} %multiply_convert_fusion), channel_id=1, source_target_pairs={{0,1},{1,2},{2,3},{3,0},{4,5},{5,6},{6,7},{7,4},{8,9},{9,10},{10,1... | collective-permute-start | bytes 3538952 | tf_op jit(solution)/shard_map/ppermute | solution.py:81
  176.2 96.2 %collective-permute-start.22 = (bf16[512,1152]{1,0:T(8,128)(2,1)S(1)}, bf16[512,1152]{1,0:T(8,128)(2,1)S(1)}, u32[]{:S(2)}, u32[]{:S(2)}) collective-permute-start(bf16[512,1152]{1,0:T(8,128)(2,1)S(1)} %multiply_convert_fusion), channel_id=1, source_target_pairs={{0,2},{1,3},{2,0},{3,1},{4,6},{5,7},{6,4},{7,5},{8,10},{9,11},{10,... | collective-permute-start | bytes 3538952 | tf_op jit(solution)/shard_map/ppermute | solution.py:81
  178.8 106.5 %copy-start.25 = (bf16[4,2,144,2304]{3,2,1,0:T(8,128)(2,1)}, bf16[4,2,144,2304]{3,2,1,0:T(8,128)(2,1)S(1)}, u32[]{:S(2)}) copy-start(bf16[4,2,144,2304]{3,2,1,0:T(8,128)(2,1)S(1)} %bitcast_dynamic-update-slice_fusion.1) | copy-start | bytes 15925252
  246.5 34.1 %collective-permute-start.25 = (bf16[512,1152]{1,0:T(8,128)(2,1)S(1)}, bf16[512,1152]{1,0:T(8,128)(2,1)S(1)}, u32[]{:S(2)}, u32[]{:S(2)}) collective-permute-start(bf16[512,1152]{1,0:T(8,128)(2,1)S(1)} %multiply_convert_fusion), channel_id=1, source_target_pairs={{0,3},{1,0},{2,1},{3,2},{4,7},{5,4},{6,5},{7,6},{8,11},{9,8},{10,9... | collective-permute-start | bytes 3538952 | tf_op jit(solution)/shard_map/ppermute | solution.py:81
  254.7 61.5 %collective-permute-start.20 = (bf16[512,1152]{1,0:T(8,128)(2,1)}, bf16[512,1152]{1,0:T(8,128)(2,1)}, u32[]{:S(2)}, u32[]{:S(2)}) collective-permute-start(bf16[512,1152]{1,0:T(8,128)(2,1)} %convolution_convert_fusion.9), channel_id=1, source_target_pairs={{0,3},{1,0},{2,1},{3,2},{4,7},{5,4},{6,5},{7,6},{8,11},{9,8},{10,9... | collective-permute-start | bytes 3538952 | tf_op jit(solution)/shard_map/ppermute | solution.py:81
  280.5 52.6 %collective-permute-start.23 = (bf16[512,1152]{1,0:T(8,128)(2,1)}, bf16[512,1152]{1,0:T(8,128)(2,1)}, u32[]{:S(2)}, u32[]{:S(2)}) collective-permute-start(bf16[512,1152]{1,0:T(8,128)(2,1)} %convolution_convert_fusion.8), channel_id=1, source_target_pairs={{0,2},{1,3},{2,0},{3,1},{4,6},{5,7},{6,4},{7,5},{8,10},{9,11},{10,... | collective-permute-start | bytes 3538952 | tf_op jit(solution)/shard_map/ppermute | solution.py:81
  288.6 44.5 %collective-permute-start.26 = (bf16[512,1152]{1,0:T(8,128)(2,1)}, bf16[512,1152]{1,0:T(8,128)(2,1)}, u32[]{:S(2)}, u32[]{:S(2)}) collective-permute-start(bf16[512,1152]{1,0:T(8,128)(2,1)} %convolution_convert_fusion.7), channel_id=1, source_target_pairs={{0,1},{1,2},{2,3},{3,0},{4,5},{5,6},{6,7},{7,4},{8,9},{9,10},{10,1... | collective-permute-start | bytes 3538952 | tf_op jit(solution)/shard_map/ppermute | solution.py:81
  303.7 38.5 %collective-permute-start.51 = (bf16[4,144,1536]{2,1,0:T(8,128)(2,1)S(1)}, bf16[4,144,1536]{2,1,0:T(8,128)(2,1)S(1)}, u32[]{:S(2)}, u32[]{:S(2)}) collective-permute-start(bf16[4,144,1536]{2,1,0:T(8,128)(2,1)S(1)} %dynamic-slice_bitcast_fusion), channel_id=1, source_target_pairs={{0,4},{4,0},{1,5},{5,1},{2,6},{6,2},{3,7},{7,3},{8,12},{12,8},{9,1... | collective-permute-start | bytes 5308424 | tf_op jit(solution)/shard_map/ppermute | solution.py:81
  308.8 181.2 %collective-permute-start.28 = (bf16[512,1152]{1,0:T(8,128)(2,1)}, bf16[512,1152]{1,0:T(8,128)(2,1)}, u32[]{:S(2)}, u32[]{:S(2)}) collective-permute-start(bf16[512,1152]{1,0:T(8,128)(2,1)} %convolution_convert_fusion.6), channel_id=1, source_target_pairs={{0,3},{1,0},{2,1},{3,2},{4,7},{5,4},{6,5},{7,6},{8,11},{9,8},{10,9... | collective-permute-start | bytes 3538952 | tf_op jit(solution)/shard_map/ppermute | solution.py:81
  340.2 46.3 %collective-permute-start.27 = (bf16[1,512,1152]{2,1,0:T(8,128)(2,1)S(1)}, bf16[1,512,1152]{2,1,0:T(8,128)(2,1)S(1)}, u32[]{:S(2)}, u32[]{:S(2)}) collective-permute-start(bf16[1,512,1152]{2,1,0:T(8,128)(2,1)S(1)} %get-tuple-element.35), channel_id=1, source_target_pairs={{0,4},{4,0},{1,5},{5,1},{2,6},{6,2},{3,7},{7,3},{8,12},{12,8},{9,1... | collective-permute-start | bytes 3538952 | tf_op jit(solution)/shard_map/ppermute | solution.py:81
  342.9 11.7 %collective-permute-start.52 = (bf16[144,1536]{1,0:T(8,128)(2,1)S(1)}, bf16[144,1536]{1,0:T(8,128)(2,1)S(1)}, u32[]{:S(2)}, u32[]{:S(2)}) collective-permute-start(bf16[144,1536]{1,0:T(8,128)(2,1)S(1)} %get-tuple-element.51), channel_id=1, source_target_pairs={{0,8},{8,16},{16,24},{24,0},{1,9},{9,17},{17,25},{25,1},{2,10},{10... | collective-permute-start | bytes 1327112 | tf_op jit(solution)/shard_map/ppermute | solution.py:81
  343.0 38.1 %collective-permute-start.53 = (bf16[144,1536]{1,0:T(8,128)(2,1)S(1)}, bf16[144,1536]{1,0:T(8,128)(2,1)S(1)}, u32[]{:S(2)}, u32[]{:S(2)}) collective-permute-start(bf16[144,1536]{1,0:T(8,128)(2,1)S(1)} %get-tuple-element.53), channel_id=1, source_target_pairs={{0,16},{8,24},{16,0},{24,8},{1,17},{9,25},{17,1},{25,9},{2,18},{10... | collective-permute-start | bytes 1327112 | tf_op jit(solution)/shard_map/ppermute | solution.py:81
  346.2 39.1 %collective-permute-start.54 = (bf16[144,1536]{1,0:T(8,128)(2,1)S(1)}, bf16[144,1536]{1,0:T(8,128)(2,1)S(1)}, u32[]{:S(2)}, u32[]{:S(2)}) collective-permute-start(bf16[144,1536]{1,0:T(8,128)(2,1)S(1)} %get-tuple-element.52), channel_id=1, source_target_pairs={{0,24},{8,0},{16,8},{24,16},{1,25},{9,1},{17,9},{25,17},{2,26},{10... | collective-permute-start | bytes 1327112 | tf_op jit(solution)/shard_map/ppermute | solution.py:81
  354.6 135.5 %collective-permute-start.29 = (bf16[512,1152]{1,0:T(8,128)(2,1)}, bf16[512,1152]{1,0:T(8,128)(2,1)}, u32[]{:S(2)}, u32[]{:S(2)}) collective-permute-start(bf16[512,1152]{1,0:T(8,128)(2,1)} %convolution_convert_fusion.5), channel_id=1, source_target_pairs={{0,2},{1,3},{2,0},{3,1},{4,6},{5,7},{6,4},{7,5},{8,10},{9,11},{10,... | collective-permute-start | bytes 3538952 | tf_op jit(solution)/shard_map/ppermute | solution.py:81
  381.1 109.0 %collective-permute-start.30 = (bf16[512,1152]{1,0:T(8,128)(2,1)}, bf16[512,1152]{1,0:T(8,128)(2,1)}, u32[]{:S(2)}, u32[]{:S(2)}) collective-permute-start(bf16[512,1152]{1,0:T(8,128)(2,1)} %convolution_convert_fusion.4), channel_id=1, source_target_pairs={{0,1},{1,2},{2,3},{3,0},{4,5},{5,6},{6,7},{7,4},{8,9},{9,10},{10,1... | collective-permute-start | bytes 3538952 | tf_op jit(solution)/shard_map/ppermute | solution.py:81
  469.1 27.4 %collective-permute-start.44 = (f32[1152,2]{0,1:T(2,128)}, f32[1152,2]{0,1:T(2,128)}, u32[]{:S(2)}, u32[]{:S(2)}) collective-permute-start(f32[1152,2]{0,1:T(2,128)} %pad_maximum_fusion.5), channel_id=1, source_target_pairs={{0,4},{4,0},{1,5},{5,1},{2,6},{6,2},{3,7},{7,3},{8,12},{12,8},{9,1... | collective-permute-start | bytes 27656 | tf_op jit(solution)/shard_map/ppermute | solution.py:81
  472.8 36.9 %collective-permute-start.38 = (bf16[4,72,576]{2,1,0:T(8,128)(2,1)}, bf16[4,72,576]{2,1,0:T(8,128)(2,1)}, u32[]{:S(2)}, u32[]{:S(2)}) collective-permute-start(bf16[4,72,576]{2,1,0:T(8,128)(2,1)} %get-tuple-element.68), channel_id=1, source_target_pairs={{0,1},{1,2},{2,3},{3,0},{4,5},{5,6},{6,7},{7,4},{8,9},{9,10},{10,1... | collective-permute-start | bytes 995336 | tf_op jit(solution)/shard_map/ppermute | solution.py:81
  490.0 22.2 %collective-permute-start.39 = (bf16[4,72,576]{2,1,0:T(8,128)(2,1)}, bf16[4,72,576]{2,1,0:T(8,128)(2,1)}, u32[]{:S(2)}, u32[]{:S(2)}) collective-permute-start(bf16[4,72,576]{2,1,0:T(8,128)(2,1)} %get-tuple-element.70), channel_id=1, source_target_pairs={{0,2},{1,3},{2,0},{3,1},{4,6},{5,7},{6,4},{7,5},{8,10},{9,11},{10,... | collective-permute-start | bytes 995336 | tf_op jit(solution)/shard_map/ppermute | solution.py:81
  498.7 3.2 collective-permute-start.47
  500.9 2.4 collective-permute-start.46
  501.8 3.3 collective-permute-start.45
  505.2 2.4 collective-permute-start.48
  505.3 3.4 collective-permute-start.49
  505.4 3.7 collective-permute-start.50
  507.6 8.5 %collective-permute-start.40 = (bf16[4,72,576]{2,1,0:T(8,128)(2,1)}, bf16[4,72,576]{2,1,0:T(8,128)(2,1)S(1)}, u32[]{:S(2)}, u32[]{:S(2)}) collective-permute-start(bf16[4,72,576]{2,1,0:T(8,128)(2,1)} %get-tuple-element.69), channel_id=1, source_target_pairs={{0,3},{1,0},{2,1},{3,2},{4,7},{5,4},{6,5},{7,6},{8,11},{9,8},{10,9... | collective-permute-start | bytes 995336 | tf_op jit(solution)/shard_map/ppermute | solution.py:81
  508.7 19.1 %collective-permute-start.32 = (bf16[4,72,960]{2,1,0:T(8,128)(2,1)}, bf16[4,72,960]{2,1,0:T(8,128)(2,1)S(1)}, u32[]{:S(2)}, u32[]{:S(2)}) collective-permute-start(bf16[4,72,960]{2,1,0:T(8,128)(2,1)} %get-tuple-element.58), channel_id=1, source_target_pairs={{0,1},{1,2},{2,3},{3,0},{4,5},{5,6},{6,7},{7,4},{8,9},{9,10},{10,1... | collective-permute-start | bytes 1658888 | tf_op jit(solution)/shard_map/ppermute | solution.py:81
  509.1 22.7 %collective-permute-start.33 = (bf16[4,72,960]{2,1,0:T(8,128)(2,1)}, bf16[4,72,960]{2,1,0:T(8,128)(2,1)S(1)}, u32[]{:S(2)}, u32[]{:S(2)}) collective-permute-start(bf16[4,72,960]{2,1,0:T(8,128)(2,1)} %get-tuple-element.60), channel_id=1, source_target_pairs={{0,2},{1,3},{2,0},{3,1},{4,6},{5,7},{6,4},{7,5},{8,10},{9,11},{10,... | collective-permute-start | bytes 1658888 | tf_op jit(solution)/shard_map/ppermute | solution.py:81
  509.7 30.0 %collective-permute-start.34 = (bf16[4,72,960]{2,1,0:T(8,128)(2,1)}, bf16[4,72,960]{2,1,0:T(8,128)(2,1)S(1)}, u32[]{:S(2)}, u32[]{:S(2)}) collective-permute-start(bf16[4,72,960]{2,1,0:T(8,128)(2,1)} %get-tuple-element.59), channel_id=1, source_target_pairs={{0,3},{1,0},{2,1},{3,2},{4,7},{5,4},{6,5},{7,6},{8,11},{9,8},{10,9... | collective-permute-start | bytes 1658888 | tf_op jit(solution)/shard_map/ppermute | solution.py:81
  512.2 46.3 %collective-permute-start.55 = (bf16[4,144,768]{2,1,0:T(8,128)(2,1)}, bf16[4,144,768]{2,1,0:T(8,128)(2,1)S(1)}, u32[]{:S(2)}, u32[]{:S(2)}) collective-permute-start(bf16[4,144,768]{2,1,0:T(8,128)(2,1)} %dynamic-slice_bitcast_fusion.3), channel_id=1, source_target_pairs={{0,4},{4,0},{1,5},{5,1},{2,6},{6,2},{3,7},{7,3},{8,12},{12,8},{9,1... | collective-permute-start | bytes 2654216 | tf_op jit(solution)/shard_map/ppermute | solution.py:81
  516.2 64.9 %collective-permute-start.31 = (bf16[1,512,1152]{2,1,0:T(8,128)(2,1)S(1)}, bf16[1,512,1152]{2,1,0:T(8,128)(2,1)S(1)}, u32[]{:S(2)}, u32[]{:S(2)}) collective-permute-start(bf16[1,512,1152]{2,1,0:T(8,128)(2,1)S(1)} %dynamic-slice_bitcast_fusion.1), channel_id=1, source_target_pairs={{0,4},{4,0},{1,5},{5,1},{2,6},{6,2},{3,7},{7,3},{8,12},{12,8},{9,1... | collective-permute-start | bytes 3538952 | tf_op jit(solution)/shard_map/ppermute | solution.py:81
  527.7 14.4 %collective-permute-start.41 = (bf16[72,576]{1,0:T(8,128)(2,1)S(1)}, bf16[72,576]{1,0:T(8,128)(2,1)S(1)}, u32[]{:S(2)}, u32[]{:S(2)}) collective-permute-start(bf16[72,576]{1,0:T(8,128)(2,1)S(1)} %get-tuple-element.76), channel_id=1, source_target_pairs={{0,8},{8,16},{16,24},{24,0},{1,9},{9,17},{17,25},{25,1},{2,10},{10... | collective-permute-start | bytes 248840 | tf_op jit(solution)/shard_map/ppermute | solution.py:81
  531.9 10.3 %collective-permute-start.42 = (bf16[72,576]{1,0:T(8,128)(2,1)S(1)}, bf16[72,576]{1,0:T(8,128)(2,1)S(1)}, u32[]{:S(2)}, u32[]{:S(2)}) collective-permute-start(bf16[72,576]{1,0:T(8,128)(2,1)S(1)} %get-tuple-element.78), channel_id=1, source_target_pairs={{0,16},{8,24},{16,0},{24,8},{1,17},{9,25},{17,1},{25,9},{2,18},{10... | collective-permute-start | bytes 248840 | tf_op jit(solution)/shard_map/ppermute | solution.py:81
  539.7 5.7 collective-permute-start.43
  542.1 4.5 collective-permute-start.35
  542.2 12.2 %collective-permute-start.36 = (bf16[72,960]{1,0:T(8,128)(2,1)S(1)}, bf16[72,960]{1,0:T(8,128)(2,1)S(1)}, u32[]{:S(2)}, u32[]{:S(2)}) collective-permute-start(bf16[72,960]{1,0:T(8,128)(2,1)S(1)} %get-tuple-element.73), channel_id=1, source_target_pairs={{0,16},{8,24},{16,0},{24,8},{1,17},{9,25},{17,1},{25,9},{2,18},{10... | collective-permute-start | bytes 414728 | tf_op jit(solution)/shard_map/ppermute | solution.py:81
  545.4 12.3 %collective-permute-start.37 = (bf16[72,960]{1,0:T(8,128)(2,1)S(1)}, bf16[72,960]{1,0:T(8,128)(2,1)S(1)}, u32[]{:S(2)}, u32[]{:S(2)}) collective-permute-start(bf16[72,960]{1,0:T(8,128)(2,1)S(1)} %get-tuple-element.72), channel_id=1, source_target_pairs={{0,24},{8,0},{16,8},{24,16},{1,25},{9,1},{17,9},{25,17},{2,26},{10... | collective-permute-start | bytes 414728 | tf_op jit(solution)/shard_map/ppermute | solution.py:81
  558.8 4.8 collective-permute-start.56
  558.8 16.8 %collective-permute-start.57 = (bf16[144,768]{1,0:T(8,128)(2,1)S(1)}, bf16[144,768]{1,0:T(8,128)(2,1)S(1)}, u32[]{:S(2)}, u32[]{:S(2)}) collective-permute-start(bf16[144,768]{1,0:T(8,128)(2,1)S(1)} %get-tuple-element.63), channel_id=1, source_target_pairs={{0,16},{8,24},{16,0},{24,8},{1,17},{9,25},{17,1},{25,9},{2,18},{10... | collective-permute-start | bytes 663560 | tf_op jit(solution)/shard_map/ppermute | solution.py:81
  560.1 20.1 %collective-permute-start.58 = (bf16[144,768]{1,0:T(8,128)(2,1)S(1)}, bf16[144,768]{1,0:T(8,128)(2,1)S(1)}, u32[]{:S(2)}, u32[]{:S(2)}) collective-permute-start(bf16[144,768]{1,0:T(8,128)(2,1)S(1)} %get-tuple-element.62), channel_id=1, source_target_pairs={{0,24},{8,0},{16,8},{24,16},{1,25},{9,1},{17,9},{25,17},{2,26},{10... | collective-permute-start | bytes 663560 | tf_op jit(solution)/shard_map/ppermute | solution.py:81
  (78 other events, 515.5 us)
